TPU v7x, 32 devices: a whole 2x2x4 slice. The times are simulated.
32 devices in a mesh: groups: 2 (over x), tm: 16 (over z, y, core).
Axes of the slice: x: 2, y: 2, z: 4, core: 2. Of those that a mesh axis runs over, the one named last changes fastest.
Arguments:
- lin_mean: float32 [128, 512], P(('groups', 'tm')), parts along dimension 0, may hold values from -6 to 6
- spread: float32 [128, 512], P(('groups', 'tm')), parts along dimension 0, may hold values from 0.05 to 0.5
- keep: float32 [128, 512], P(('groups', 'tm')), parts along dimension 0, may hold values from 0.3 to 1
- observed: float32 [128, 512], P(('groups', 'tm')), parts along dimension 0, may hold values from -6 to 6
- start: float32 [1024], P('groups'), parts along dimension 0, may hold values from -6 to 6
- w_in: bfloat16 [512, 2048], replicated, may hold values from -0.176776695 to 0.176776695
- b_in: float32 [2048], replicated, may hold values from -3 to 3
- w_out: bfloat16 [2048, 512], replicated, may hold values from -0.013258252 to 0.013258252
- b_out: float32 [512], replicated, may hold values from -0.6 to 0.6
Outputs:
- filtered: float32 [128, 512], P(('groups', 'tm')), parts along dimension 0
There are 2 independent parts, one for each index of `groups`. A program takes and returns all parts, laid end to end along the dimension named above; an argument that names none is the same for every part. Nothing has to cross between parts.
All inputs are finite; a program needn't handle non-finite values.
Results may differ from a plain program's by a relative error of at most 0.0003.
The roundings to bfloat16 on the way count: a program that leaves them out, or rounds other values in their place, can miss the bound.
Values sent between devices are 32-bit elements; how exact they have to be, the bound alone decides.
No kernel may reach another device: no remote copies, remote signals or barrier semaphores. Data moves between devices by JAX's collectives and lax.ppermute only.
A program may use at most 64 MiB of HBM per device.

v0:
```python
import math

import jax
import jax.numpy as jnp
from jax import lax
from jax.sharding import PartitionSpec as P


def shifted(block, axis, distance):
    devices = range(lax.axis_size(axis))
    route = [(i - distance, i) for i in devices if i - distance in devices]
    return lax.ppermute(block, axis, route)


def forward_net(points, w_in, b_in, w_out, b_out):
    hidden = jax.nn.gelu(
        jnp.dot(points, w_in, preferred_element_type=jnp.float32) + b_in, approximate=True
    ).astype(jnp.bfloat16)
    return (
        jnp.dot(hidden, w_out, preferred_element_type=jnp.float32)
        + b_out
        + points.astype(jnp.float32)
    )


def evaluate_all(mean_rows, spread_rows, factor, w_in, b_in, w_out, b_out):
    local_steps, state_width = mean_rows.shape
    offset = (
        jnp.eye(state_width, dtype=jnp.float32)[None, :, :] * (factor * spread_rows)[:, :, None]
    )
    upper_pts = (mean_rows[:, None, :] + offset).astype(jnp.bfloat16)
    lower_pts = (mean_rows[:, None, :] - offset).astype(jnp.bfloat16)
    stacked = jnp.concatenate([upper_pts, lower_pts], axis=1).reshape(
        local_steps * 2 * state_width, state_width
    )
    everything = jnp.concatenate([stacked, mean_rows.astype(jnp.bfloat16)], axis=0)
    outputs = forward_net(everything, w_in, b_in, w_out, b_out)
    paired = outputs[: local_steps * 2 * state_width].reshape(
        local_steps, 2, state_width, state_width
    )
    centre = outputs[local_steps * 2 * state_width :]
    jacobian = (paired[:, 0] - paired[:, 1]) / (2.0 * factor * spread_rows)[:, :, None]
    point_total = jnp.sum(paired[:, 0] + paired[:, 1], axis=1)
    return (jacobian, point_total, centre)


def high_dot(left, right):
    return jnp.dot(left, right, precision=lax.Precision.HIGHEST)


def advance_step(filt_prev, inputs):
    jac_step, mean_step, lin_row, keep_row, observed_row = inputs
    predicted = mean_step + high_dot(filt_prev - lin_row, jac_step)
    new_state = keep_row * predicted + (1.0 - keep_row) * observed_row
    return (new_state, new_state)


def body(lin_mean, spread, keep, observed, start, w_in, b_in, w_out, b_out):
    local_steps, state_width = lin_mean.shape
    factor = math.sqrt(state_width + 1.0)
    jacobian, point_total, centre = evaluate_all(lin_mean, spread, factor, w_in, b_in, w_out, b_out)
    point_mean = centre / (state_width + 1.0) + point_total / (2.0 * (state_width + 1.0))
    elements = (jacobian, point_mean, lin_mean, keep, observed)
    position = lax.axis_index("tm")

    def handoff_turn(turn_index, incoming):
        final_state, unused_rows = lax.scan(advance_step, incoming, elements)
        moved_state = shifted(final_state, "tm", 1)
        return jnp.where(position == 0, start, moved_state)

    entering = lax.fori_loop(0, lax.axis_size("tm") - 1, handoff_turn, start)
    unused_last, filtered = lax.scan(advance_step, entering, elements)
    return filtered


def solution(mesh):
    placed = (
        P(("groups", "tm"), None),
        P(("groups", "tm"), None),
        P(("groups", "tm"), None),
        P(("groups", "tm"), None),
        P("groups"),
        P(),
        P(),
        P(),
        P(),
    )
    return jax.shard_map(
        body, mesh=mesh, in_specs=placed, out_specs=P(("groups", "tm"), None), check_vma=False
    )
```

profile of v0, /device:TPU:10, one launch (start us, length us, event | category | flops | bytes accessed | tf_op | source)
XLA Modules:
  0.0 257.2 jit_solution(17987033619313149112)
XLA Ops:
  4.6 29.7 %convert_add_fusion = f32[4100,512]{1,0:T(8,128)} fusion(bf16[2048,512]{1,0:T(8,128)(2,1)S(1)} %copy-done, f32[512]{0:T(512)S(1)} %copy-done.6, bf16[4,512]{1,0:T(4,128)(2,1)S(1)} %convert_element_type.25, bf16[4096,512]{1,0:T(8,128)(2,1)} %bitcast.86, bf16[512,2048]{1,0:T(8,128)(2,1)} %param.20, f32[2048]{0:T(1024)S(1)} %copy-done.5), kind=kOutput, calls=%fused_computation.28 | convolution fusion | flops 17301606400 | bytes 16799744 | tf_op jit(solution)/shard_map/dot_general | solution.py:20
  34.4 4.4 %slice.19 = f32[4096,512]{1,0:T(8,128)S(1)} slice(f32[4100,512]{1,0:T(8,128)} %convert_add_fusion), slice={[0:4096], [0:512]} | slice | bytes 16777216 | tf_op jit(solution)/shard_map/slice | solution.py:38
  42.7 201.7 %while.41 = (s32[]{:T(128)}, f32[512]{0:T(512)S(1)}, pred[]{:T(512)}, f32[4,512]{1,0:T(4,128)S(1)}, f32[4,512]{1,0:T(4,128)S(1)}, /*index=5*/f32[4,512]{1,0:T(4,...) while((s32[]{:T(128)}, f32[512]{0:T(512)S(1)}, ...), condition=%wide.region_4.5_spmd, body=%wide.region_1.4_spmd.sunk | while | flops 3149316 | bytes 1100635 | solution.py:71
  42.7 7.6 %while.43 = (s32[]{:T(128)}, f32[512]{0:T(512)S(1)}, f32[4,512]{1,0:T(4,128)S(1)}, f32[4,512]{1,0:T(4,128)S(1)}, f32[4,512]{1,0:T(4,128)S(1)}, /*index=5*/f32[4,512,512]{2,1,0:T(8,128)}, f32[4,512]{1,0:T(4,128)S(1)}, s32[]{:T(128)}) while((s32[]{:T(128)}, f32[512]{0:T(512)S(1)}, f32[4,512]{1,0:T(4,128)S(1)}, f32[4,512]{1,0:T(4,128)S(1)}, ...), condition=%wide.region_3.3_spmd, body=%wide.region_2.2_spmd.sunk | while | flops 3148802 | bytes 1086045 | solution.py:67
  52.3 3.9 %collective-permute-done = f32[512]{0:T(512)S(1)} collective-permute-done((f32[512]{0:T(512)S(1)}, f32[512]{0:T(512)S(1)}, u32[]{:S(2)}, u32[]{:S(2)}) %collective-permute-start) | collective-permute-done | bytes 2080 | tf_op jit(solution)/shard_map/while/body/eval_jaxpr/ppermute | solution.py:12
  56.2 7.6 %while.43 = (s32[]{:T(128)}, f32[512]{0:T(512)S(1)}, f32[4,512]{1,0:T(4,128)S(1)}, f32[4,512]{1,0:T(4,128)S(1)}, f32[4,512]{1,0:T(4,128)S(1)}, /*index=5*/f32[4,512,512]{2,1,0:T(8,128)}, f32[4,512]{1,0:T(4,128)S(1)}, s32[]{:T(128)}) while((s32[]{:T(128)}, f32[512]{0:T(512)S(1)}, f32[4,512]{1,0:T(4,128)S(1)}, f32[4,512]{1,0:T(4,128)S(1)}, ...), condition=%wide.region_3.3_spmd, body=%wide.region_2.2_spmd.sunk | while | flops 3148802 | bytes 1086045 | solution.py:67
  65.7 3.9 %collective-permute-done = f32[512]{0:T(512)S(1)} collective-permute-done((f32[512]{0:T(512)S(1)}, f32[512]{0:T(512)S(1)}, u32[]{:S(2)}, u32[]{:S(2)}) %collective-permute-start) | collective-permute-done | bytes 2080 | tf_op jit(solution)/shard_map/while/body/eval_jaxpr/ppermute | solution.py:12
  69.6 7.6 %while.43 = (s32[]{:T(128)}, f32[512]{0:T(512)S(1)}, f32[4,512]{1,0:T(4,128)S(1)}, f32[4,512]{1,0:T(4,128)S(1)}, f32[4,512]{1,0:T(4,128)S(1)}, /*index=5*/f32[4,512,512]{2,1,0:T(8,128)}, f32[4,512]{1,0:T(4,128)S(1)}, s32[]{:T(128)}) while((s32[]{:T(128)}, f32[512]{0:T(512)S(1)}, f32[4,512]{1,0:T(4,128)S(1)}, f32[4,512]{1,0:T(4,128)S(1)}, ...), condition=%wide.region_3.3_spmd, body=%wide.region_2.2_spmd.sunk | while | flops 3148802 | bytes 1086045 | solution.py:67
  83.0 7.6 %while.43 = (s32[]{:T(128)}, f32[512]{0:T(512)S(1)}, f32[4,512]{1,0:T(4,128)S(1)}, f32[4,512]{1,0:T(4,128)S(1)}, f32[4,512]{1,0:T(4,128)S(1)}, /*index=5*/f32[4,512,512]{2,1,0:T(8,128)}, f32[4,512]{1,0:T(4,128)S(1)}, s32[]{:T(128)}) while((s32[]{:T(128)}, f32[512]{0:T(512)S(1)}, f32[4,512]{1,0:T(4,128)S(1)}, f32[4,512]{1,0:T(4,128)S(1)}, ...), condition=%wide.region_3.3_spmd, body=%wide.region_2.2_spmd.sunk | while | flops 3148802 | bytes 1086045 | solution.py:67
  92.6 3.9 %collective-permute-done = f32[512]{0:T(512)S(1)} collective-permute-done((f32[512]{0:T(512)S(1)}, f32[512]{0:T(512)S(1)}, u32[]{:S(2)}, u32[]{:S(2)}) %collective-permute-start) | collective-permute-done | bytes 2080 | tf_op jit(solution)/shard_map/while/body/eval_jaxpr/ppermute | solution.py:12
  96.5 7.6 %while.43 = (s32[]{:T(128)}, f32[512]{0:T(512)S(1)}, f32[4,512]{1,0:T(4,128)S(1)}, f32[4,512]{1,0:T(4,128)S(1)}, f32[4,512]{1,0:T(4,128)S(1)}, /*index=5*/f32[4,512,512]{2,1,0:T(8,128)}, f32[4,512]{1,0:T(4,128)S(1)}, s32[]{:T(128)}) while((s32[]{:T(128)}, f32[512]{0:T(512)S(1)}, f32[4,512]{1,0:T(4,128)S(1)}, f32[4,512]{1,0:T(4,128)S(1)}, ...), condition=%wide.region_3.3_spmd, body=%wide.region_2.2_spmd.sunk | while | flops 3148802 | bytes 1086045 | solution.py:67
  106.0 3.9 %collective-permute-done = f32[512]{0:T(512)S(1)} collective-permute-done((f32[512]{0:T(512)S(1)}, f32[512]{0:T(512)S(1)}, u32[]{:S(2)}, u32[]{:S(2)}) %collective-permute-start) | collective-permute-done | bytes 2080 | tf_op jit(solution)/shard_map/while/body/eval_jaxpr/ppermute | solution.py:12
  109.9 7.6 %while.43 = (s32[]{:T(128)}, f32[512]{0:T(512)S(1)}, f32[4,512]{1,0:T(4,128)S(1)}, f32[4,512]{1,0:T(4,128)S(1)}, f32[4,512]{1,0:T(4,128)S(1)}, /*index=5*/f32[4,512,512]{2,1,0:T(8,128)}, f32[4,512]{1,0:T(4,128)S(1)}, s32[]{:T(128)}) while((s32[]{:T(128)}, f32[512]{0:T(512)S(1)}, f32[4,512]{1,0:T(4,128)S(1)}, f32[4,512]{1,0:T(4,128)S(1)}, ...), condition=%wide.region_3.3_spmd, body=%wide.region_2.2_spmd.sunk | while | flops 3148802 | bytes 1086045 | solution.py:67
  119.5 3.9 %collective-permute-done = f32[512]{0:T(512)S(1)} collective-permute-done((f32[512]{0:T(512)S(1)}, f32[512]{0:T(512)S(1)}, u32[]{:S(2)}, u32[]{:S(2)}) %collective-permute-start) | collective-permute-done | bytes 2080 | tf_op jit(solution)/shard_map/while/body/eval_jaxpr/ppermute | solution.py:12
  123.4 7.6 %while.43 = (s32[]{:T(128)}, f32[512]{0:T(512)S(1)}, f32[4,512]{1,0:T(4,128)S(1)}, f32[4,512]{1,0:T(4,128)S(1)}, f32[4,512]{1,0:T(4,128)S(1)}, /*index=5*/f32[4,512,512]{2,1,0:T(8,128)}, f32[4,512]{1,0:T(4,128)S(1)}, s32[]{:T(128)}) while((s32[]{:T(128)}, f32[512]{0:T(512)S(1)}, f32[4,512]{1,0:T(4,128)S(1)}, f32[4,512]{1,0:T(4,128)S(1)}, ...), condition=%wide.region_3.3_spmd, body=%wide.region_2.2_spmd.sunk | while | flops 3148802 | bytes 1086045 | solution.py:67
  132.9 3.9 %collective-permute-done = f32[512]{0:T(512)S(1)} collective-permute-done((f32[512]{0:T(512)S(1)}, f32[512]{0:T(512)S(1)}, u32[]{:S(2)}, u32[]{:S(2)}) %collective-permute-start) | collective-permute-done | bytes 2080 | tf_op jit(solution)/shard_map/while/body/eval_jaxpr/ppermute | solution.py:12
  136.8 7.6 %while.43 = (s32[]{:T(128)}, f32[512]{0:T(512)S(1)}, f32[4,512]{1,0:T(4,128)S(1)}, f32[4,512]{1,0:T(4,128)S(1)}, f32[4,512]{1,0:T(4,128)S(1)}, /*index=5*/f32[4,512,512]{2,1,0:T(8,128)}, f32[4,512]{1,0:T(4,128)S(1)}, s32[]{:T(128)}) while((s32[]{:T(128)}, f32[512]{0:T(512)S(1)}, f32[4,512]{1,0:T(4,128)S(1)}, f32[4,512]{1,0:T(4,128)S(1)}, ...), condition=%wide.region_3.3_spmd, body=%wide.region_2.2_spmd.sunk | while | flops 3148802 | bytes 1086045 | solution.py:67
  146.4 3.9 %collective-permute-done = f32[512]{0:T(512)S(1)} collective-permute-done((f32[512]{0:T(512)S(1)}, f32[512]{0:T(512)S(1)}, u32[]{:S(2)}, u32[]{:S(2)}) %collective-permute-start) | collective-permute-done | bytes 2080 | tf_op jit(solution)/shard_map/while/body/eval_jaxpr/ppermute | solution.py:12
  150.3 7.6 %while.43 = (s32[]{:T(128)}, f32[512]{0:T(512)S(1)}, f32[4,512]{1,0:T(4,128)S(1)}, f32[4,512]{1,0:T(4,128)S(1)}, f32[4,512]{1,0:T(4,128)S(1)}, /*index=5*/f32[4,512,512]{2,1,0:T(8,128)}, f32[4,512]{1,0:T(4,128)S(1)}, s32[]{:T(128)}) while((s32[]{:T(128)}, f32[512]{0:T(512)S(1)}, f32[4,512]{1,0:T(4,128)S(1)}, f32[4,512]{1,0:T(4,128)S(1)}, ...), condition=%wide.region_3.3_spmd, body=%wide.region_2.2_spmd.sunk | while | flops 3148802 | bytes 1086045 | solution.py:67
  159.8 3.9 %collective-permute-done = f32[512]{0:T(512)S(1)} collective-permute-done((f32[512]{0:T(512)S(1)}, f32[512]{0:T(512)S(1)}, u32[]{:S(2)}, u32[]{:S(2)}) %collective-permute-start) | collective-permute-done | bytes 2080 | tf_op jit(solution)/shard_map/while/body/eval_jaxpr/ppermute | solution.py:12
  163.7 7.6 %while.43 = (s32[]{:T(128)}, f32[512]{0:T(512)S(1)}, f32[4,512]{1,0:T(4,128)S(1)}, f32[4,512]{1,0:T(4,128)S(1)}, f32[4,512]{1,0:T(4,128)S(1)}, /*index=5*/f32[4,512,512]{2,1,0:T(8,128)}, f32[4,512]{1,0:T(4,128)S(1)}, s32[]{:T(128)}) while((s32[]{:T(128)}, f32[512]{0:T(512)S(1)}, f32[4,512]{1,0:T(4,128)S(1)}, f32[4,512]{1,0:T(4,128)S(1)}, ...), condition=%wide.region_3.3_spmd, body=%wide.region_2.2_spmd.sunk | while | flops 3148802 | bytes 1086045 | solution.py:67
  173.3 3.9 %collective-permute-done = f32[512]{0:T(512)S(1)} collective-permute-done((f32[512]{0:T(512)S(1)}, f32[512]{0:T(512)S(1)}, u32[]{:S(2)}, u32[]{:S(2)}) %collective-permute-start) | collective-permute-done | bytes 2080 | tf_op jit(solution)/shard_map/while/body/eval_jaxpr/ppermute | solution.py:12
  177.1 7.6 %while.43 = (s32[]{:T(128)}, f32[512]{0:T(512)S(1)}, f32[4,512]{1,0:T(4,128)S(1)}, f32[4,512]{1,0:T(4,128)S(1)}, f32[4,512]{1,0:T(4,128)S(1)}, /*index=5*/f32[4,512,512]{2,1,0:T(8,128)}, f32[4,512]{1,0:T(4,128)S(1)}, s32[]{:T(128)}) while((s32[]{:T(128)}, f32[512]{0:T(512)S(1)}, f32[4,512]{1,0:T(4,128)S(1)}, f32[4,512]{1,0:T(4,128)S(1)}, ...), condition=%wide.region_3.3_spmd, body=%wide.region_2.2_spmd.sunk | while | flops 3148802 | bytes 1086045 | solution.py:67
  186.7 3.9 %collective-permute-done = f32[512]{0:T(512)S(1)} collective-permute-done((f32[512]{0:T(512)S(1)}, f32[512]{0:T(512)S(1)}, u32[]{:S(2)}, u32[]{:S(2)}) %collective-permute-start) | collective-permute-done | bytes 2080 | tf_op jit(solution)/shard_map/while/body/eval_jaxpr/ppermute | solution.py:12
  190.6 7.6 %while.43 = (s32[]{:T(128)}, f32[512]{0:T(512)S(1)}, f32[4,512]{1,0:T(4,128)S(1)}, f32[4,512]{1,0:T(4,128)S(1)}, f32[4,512]{1,0:T(4,128)S(1)}, /*index=5*/f32[4,512,512]{2,1,0:T(8,128)}, f32[4,512]{1,0:T(4,128)S(1)}, s32[]{:T(128)}) while((s32[]{:T(128)}, f32[512]{0:T(512)S(1)}, f32[4,512]{1,0:T(4,128)S(1)}, f32[4,512]{1,0:T(4,128)S(1)}, ...), condition=%wide.region_3.3_spmd, body=%wide.region_2.2_spmd.sunk | while | flops 3148802 | bytes 1086045 | solution.py:67
  204.0 7.6 %while.43 = (s32[]{:T(128)}, f32[512]{0:T(512)S(1)}, f32[4,512]{1,0:T(4,128)S(1)}, f32[4,512]{1,0:T(4,128)S(1)}, f32[4,512]{1,0:T(4,128)S(1)}, /*index=5*/f32[4,512,512]{2,1,0:T(8,128)}, f32[4,512]{1,0:T(4,128)S(1)}, s32[]{:T(128)}) while((s32[]{:T(128)}, f32[512]{0:T(512)S(1)}, f32[4,512]{1,0:T(4,128)S(1)}, f32[4,512]{1,0:T(4,128)S(1)}, ...), condition=%wide.region_3.3_spmd, body=%wide.region_2.2_spmd.sunk | while | flops 3148802 | bytes 1086045 | solution.py:67
  213.6 3.9 %collective-permute-done = f32[512]{0:T(512)S(1)} collective-permute-done((f32[512]{0:T(512)S(1)}, f32[512]{0:T(512)S(1)}, u32[]{:S(2)}, u32[]{:S(2)}) %collective-permute-start) | collective-permute-done | bytes 2080 | tf_op jit(solution)/shard_map/while/body/eval_jaxpr/ppermute | solution.py:12
  217.5 7.6 %while.43 = (s32[]{:T(128)}, f32[512]{0:T(512)S(1)}, f32[4,512]{1,0:T(4,128)S(1)}, f32[4,512]{1,0:T(4,128)S(1)}, f32[4,512]{1,0:T(4,128)S(1)}, /*index=5*/f32[4,512,512]{2,1,0:T(8,128)}, f32[4,512]{1,0:T(4,128)S(1)}, s32[]{:T(128)}) while((s32[]{:T(128)}, f32[512]{0:T(512)S(1)}, f32[4,512]{1,0:T(4,128)S(1)}, f32[4,512]{1,0:T(4,128)S(1)}, ...), condition=%wide.region_3.3_spmd, body=%wide.region_2.2_spmd.sunk | while | flops 3148802 | bytes 1086045 | solution.py:67
  227.0 3.9 %collective-permute-done = f32[512]{0:T(512)S(1)} collective-permute-done((f32[512]{0:T(512)S(1)}, f32[512]{0:T(512)S(1)}, u32[]{:S(2)}, u32[]{:S(2)}) %collective-permute-start) | collective-permute-done | bytes 2080 | tf_op jit(solution)/shard_map/while/body/eval_jaxpr/ppermute | solution.py:12
  230.9 7.6 %while.43 = (s32[]{:T(128)}, f32[512]{0:T(512)S(1)}, f32[4,512]{1,0:T(4,128)S(1)}, f32[4,512]{1,0:T(4,128)S(1)}, f32[4,512]{1,0:T(4,128)S(1)}, /*index=5*/f32[4,512,512]{2,1,0:T(8,128)}, f32[4,512]{1,0:T(4,128)S(1)}, s32[]{:T(128)}) while((s32[]{:T(128)}, f32[512]{0:T(512)S(1)}, f32[4,512]{1,0:T(4,128)S(1)}, f32[4,512]{1,0:T(4,128)S(1)}, ...), condition=%wide.region_3.3_spmd, body=%wide.region_2.2_spmd.sunk | while | flops 3148802 | bytes 1086045 | solution.py:67
  240.5 3.9 %collective-permute-done = f32[512]{0:T(512)S(1)} collective-permute-done((f32[512]{0:T(512)S(1)}, f32[512]{0:T(512)S(1)}, u32[]{:S(2)}, u32[]{:S(2)}) %collective-permute-start) | collective-permute-done | bytes 2080 | tf_op jit(solution)/shard_map/while/body/eval_jaxpr/ppermute | solution.py:12
  244.4 12.9 %while.42 = (s32[]{:T(128)}, f32[512]{0:T(512)S(1)}, f32[4,512]{1,0:T(4,128)}, f32[4,512]{1,0:T(4,128)S(1)}, f32[4,512]{1,0:T(4,128)S(1)}, /*index=5*/f32[4,512]...) while((s32[]{:T(128)}, f32[512]{0:T(512)S(1)}, f32[4,512]{1,0:T(4,128)}, ...), condition=%wide.region_6.7_spmd, body=%wide.region_5.6_spmd.sunk | while | flops 3148802 | bytes 1090161 | solution.py:72
  (380 shorter events, 170.1 us)
Async XLA Ops:
  0.0 4.6 %copy-start = (bf16[2048,512]{1,0:T(8,128)(2,1)S(1)}, bf16[2048,512]{1,0:T(8,128)(2,1)}, u32[]{:S(2)}) copy-start(bf16[2048,512]{1,0:T(8,128)(2,1)} %param.22) | copy-start | bytes 6291460
  2.3 2.3 copy-start.1
  2.4 2.3 copy-start.5
  2.4 2.3 copy-start.6
  40.2 2.5 copy-start.4
  40.2 2.5 copy-start.2
  40.2 2.5 copy-start.3
  50.3 5.8 %collective-permute-start = (f32[512]{0:T(512)S(1)}, f32[512]{0:T(512)S(1)}, u32[]{:S(2)}, u32[]{:S(2)}) collective-permute-start(f32[512]{0:T(512)S(1)} %get-tuple-element.406), channel_id=1, source_target_pairs={{0,1},{1,2},{2,3},{3,4},{4,5},{5,6},{6,7},{7,8},{8,9},{9,10},{10,1... | collective-permute-start | bytes 6152 | tf_op jit(solution)/shard_map/while/body/eval_jaxpr/ppermute | solution.py:12
  63.8 5.8 %collective-permute-start = (f32[512]{0:T(512)S(1)}, f32[512]{0:T(512)S(1)}, u32[]{:S(2)}, u32[]{:S(2)}) collective-permute-start(f32[512]{0:T(512)S(1)} %get-tuple-element.406), channel_id=1, source_target_pairs={{0,1},{1,2},{2,3},{3,4},{4,5},{5,6},{6,7},{7,8},{8,9},{9,10},{10,1... | collective-permute-start | bytes 6152 | tf_op jit(solution)/shard_map/while/body/eval_jaxpr/ppermute | solution.py:12
  77.2 5.8 %collective-permute-start = (f32[512]{0:T(512)S(1)}, f32[512]{0:T(512)S(1)}, u32[]{:S(2)}, u32[]{:S(2)}) collective-permute-start(f32[512]{0:T(512)S(1)} %get-tuple-element.406), channel_id=1, source_target_pairs={{0,1},{1,2},{2,3},{3,4},{4,5},{5,6},{6,7},{7,8},{8,9},{9,10},{10,1... | collective-permute-start | bytes 6152 | tf_op jit(solution)/shard_map/while/body/eval_jaxpr/ppermute | solution.py:12
  90.7 5.8 %collective-permute-start = (f32[512]{0:T(512)S(1)}, f32[512]{0:T(512)S(1)}, u32[]{:S(2)}, u32[]{:S(2)}) collective-permute-start(f32[512]{0:T(512)S(1)} %get-tuple-element.406), channel_id=1, source_target_pairs={{0,1},{1,2},{2,3},{3,4},{4,5},{5,6},{6,7},{7,8},{8,9},{9,10},{10,1... | collective-permute-start | bytes 6152 | tf_op jit(solution)/shard_map/while/body/eval_jaxpr/ppermute | solution.py:12
  104.1 5.8 %collective-permute-start = (f32[512]{0:T(512)S(1)}, f32[512]{0:T(512)S(1)}, u32[]{:S(2)}, u32[]{:S(2)}) collective-permute-start(f32[512]{0:T(512)S(1)} %get-tuple-element.406), channel_id=1, source_target_pairs={{0,1},{1,2},{2,3},{3,4},{4,5},{5,6},{6,7},{7,8},{8,9},{9,10},{10,1... | collective-permute-start | bytes 6152 | tf_op jit(solution)/shard_map/while/body/eval_jaxpr/ppermute | solution.py:12
  117.6 5.8 %collective-permute-start = (f32[512]{0:T(512)S(1)}, f32[512]{0:T(512)S(1)}, u32[]{:S(2)}, u32[]{:S(2)}) collective-permute-start(f32[512]{0:T(512)S(1)} %get-tuple-element.406), channel_id=1, source_target_pairs={{0,1},{1,2},{2,3},{3,4},{4,5},{5,6},{6,7},{7,8},{8,9},{9,10},{10,1... | collective-permute-start | bytes 6152 | tf_op jit(solution)/shard_map/while/body/eval_jaxpr/ppermute | solution.py:12
  131.0 5.8 %collective-permute-start = (f32[512]{0:T(512)S(1)}, f32[512]{0:T(512)S(1)}, u32[]{:S(2)}, u32[]{:S(2)}) collective-permute-start(f32[512]{0:T(512)S(1)} %get-tuple-element.406), channel_id=1, source_target_pairs={{0,1},{1,2},{2,3},{3,4},{4,5},{5,6},{6,7},{7,8},{8,9},{9,10},{10,1... | collective-permute-start | bytes 6152 | tf_op jit(solution)/shard_map/while/body/eval_jaxpr/ppermute | solution.py:12
  144.4 5.8 %collective-permute-start = (f32[512]{0:T(512)S(1)}, f32[512]{0:T(512)S(1)}, u32[]{:S(2)}, u32[]{:S(2)}) collective-permute-start(f32[512]{0:T(512)S(1)} %get-tuple-element.406), channel_id=1, source_target_pairs={{0,1},{1,2},{2,3},{3,4},{4,5},{5,6},{6,7},{7,8},{8,9},{9,10},{10,1... | collective-permute-start | bytes 6152 | tf_op jit(solution)/shard_map/while/body/eval_jaxpr/ppermute | solution.py:12
  157.9 5.8 %collective-permute-start = (f32[512]{0:T(512)S(1)}, f32[512]{0:T(512)S(1)}, u32[]{:S(2)}, u32[]{:S(2)}) collective-permute-start(f32[512]{0:T(512)S(1)} %get-tuple-element.406), channel_id=1, source_target_pairs={{0,1},{1,2},{2,3},{3,4},{4,5},{5,6},{6,7},{7,8},{8,9},{9,10},{10,1... | collective-permute-start | bytes 6152 | tf_op jit(solution)/shard_map/while/body/eval_jaxpr/ppermute | solution.py:12
  171.3 5.8 %collective-permute-start = (f32[512]{0:T(512)S(1)}, f32[512]{0:T(512)S(1)}, u32[]{:S(2)}, u32[]{:S(2)}) collective-permute-start(f32[512]{0:T(512)S(1)} %get-tuple-element.406), channel_id=1, source_target_pairs={{0,1},{1,2},{2,3},{3,4},{4,5},{5,6},{6,7},{7,8},{8,9},{9,10},{10,1... | collective-permute-start | bytes 6152 | tf_op jit(solution)/shard_map/while/body/eval_jaxpr/ppermute | solution.py:12
  184.8 5.8 %collective-permute-start = (f32[512]{0:T(512)S(1)}, f32[512]{0:T(512)S(1)}, u32[]{:S(2)}, u32[]{:S(2)}) collective-permute-start(f32[512]{0:T(512)S(1)} %get-tuple-element.406), channel_id=1, source_target_pairs={{0,1},{1,2},{2,3},{3,4},{4,5},{5,6},{6,7},{7,8},{8,9},{9,10},{10,1... | collective-permute-start | bytes 6152 | tf_op jit(solution)/shard_map/while/body/eval_jaxpr/ppermute | solution.py:12
  198.2 5.8 %collective-permute-start = (f32[512]{0:T(512)S(1)}, f32[512]{0:T(512)S(1)}, u32[]{:S(2)}, u32[]{:S(2)}) collective-permute-start(f32[512]{0:T(512)S(1)} %get-tuple-element.406), channel_id=1, source_target_pairs={{0,1},{1,2},{2,3},{3,4},{4,5},{5,6},{6,7},{7,8},{8,9},{9,10},{10,1... | collective-permute-start | bytes 6152 | tf_op jit(solution)/shard_map/while/body/eval_jaxpr/ppermute | solution.py:12
  211.7 5.8 %collective-permute-start = (f32[512]{0:T(512)S(1)}, f32[512]{0:T(512)S(1)}, u32[]{:S(2)}, u32[]{:S(2)}) collective-permute-start(f32[512]{0:T(512)S(1)} %get-tuple-element.406), channel_id=1, source_target_pairs={{0,1},{1,2},{2,3},{3,4},{4,5},{5,6},{6,7},{7,8},{8,9},{9,10},{10,1... | collective-permute-start | bytes 6152 | tf_op jit(solution)/shard_map/while/body/eval_jaxpr/ppermute | solution.py:12
  225.1 5.8 %collective-permute-start = (f32[512]{0:T(512)S(1)}, f32[512]{0:T(512)S(1)}, u32[]{:S(2)}, u32[]{:S(2)}) collective-permute-start(f32[512]{0:T(512)S(1)} %get-tuple-element.406), channel_id=1, source_target_pairs={{0,1},{1,2},{2,3},{3,4},{4,5},{5,6},{6,7},{7,8},{8,9},{9,10},{10,1... | collective-permute-start | bytes 6152 | tf_op jit(solution)/shard_map/while/body/eval_jaxpr/ppermute | solution.py:12
  238.6 5.8 %collective-permute-start = (f32[512]{0:T(512)S(1)}, f32[512]{0:T(512)S(1)}, u32[]{:S(2)}, u32[]{:S(2)}) collective-permute-start(f32[512]{0:T(512)S(1)} %get-tuple-element.406), channel_id=1, source_target_pairs={{0,1},{1,2},{2,3},{3,4},{4,5},{5,6},{6,7},{7,8},{8,9},{9,10},{10,1... | collective-permute-start | bytes 6152 | tf_op jit(solution)/shard_map/while/body/eval_jaxpr/ppermute | solution.py:12
where the time goes:
time: 260 us; the launch traced here: 257 us
  matrix products  147 us (57%)
  waiting for transfers between devices  58.1 us (22%)
  starting transfers between devices  28.8 us (11%)
  local copies, waits for them, and re-layouts  10.8 us (4%)
  other arithmetic  9.34 us (4%)
  loops' own time  2.61 us (1%)
    dot_general x64, matrix products, high_dot(): return jnp.dot(left, right, precision=lax.Precision.HIGHEST)  118 us
    ppermute x15, waiting for transfers between devices, shifted(): return lax.ppermute(block, axis, route)  58.1 us
    dot_general x1, matrix products, forward_net(): jnp.dot(hidden, w_out, preferred_element_type=jnp.float32) + b_out  29.7 us
    ppermute x15, starting transfers between devices, shifted(): return lax.ppermute(block, axis, route)  28.8 us
    dynamic_update_slice x4, local copies, waits for them, and re-layouts, body(): unused_last, filtered = lax.scan(advance_step, entering, elements)  5.29 us
  transfers between devices with their start and end apart: 15, of which 15 were waited for; matrix products, arithmetic and copies ran while one was open for 0% of the time, Pallas kernels for 0%

commit v1 on v0

v1 whole, which is shorter than its diff:
```python
import functools
import math

import jax
import jax.numpy as jnp
from jax import lax
from jax.experimental import pallas as pl
from jax.experimental.pallas import tpu as pltpu
from jax.sharding import PartitionSpec as P

C0 = math.sqrt(2.0 / math.pi)
C1 = 0.044715 * C0
LANES = 128
F32 = jnp.float32
BF16 = jnp.bfloat16
VMEM = pl.BlockSpec(memory_space=pltpu.VMEM)


def split(x):
    hi = x.astype(BF16)
    return hi, (x - hi.astype(F32)).astype(BF16)


def product(left, right):
    lhi, llo = split(left)
    rhi, rlo = split(right)
    return jnp.dot(
        jnp.concatenate([lhi, llo, lhi], axis=1),
        jnp.concatenate([rhi, rhi, rlo], axis=0),
        preferred_element_type=F32,
    )


def columns_of(row):
    width = row.shape[1]
    return [
        jnp.transpose(jnp.broadcast_to(row[:, b : b + LANES], (LANES, LANES)))
        for b in range(0, width, LANES)
    ]


def row_times(cols, matrix):
    width = len(cols) * LANES
    parts = []
    for c in range(0, width, LANES):
        total = None
        for b in range(len(cols)):
            term = jnp.sum(
                (cols[b] * matrix(pl.ds(b * LANES, LANES), pl.ds(c, LANES))).reshape(LANES // 8, 8, LANES),
                axis=0,
            )
            total = term if total is None else total + term
        parts.append(jnp.sum(total, axis=0, keepdims=True))
    return jnp.concatenate(parts, axis=1)


def net_kernel(
    mean_ref, spread_ref, keep_ref, obs_ref, w_in, b_in, w_out, b_out,
    pre, last, offsets,
    base, wide, h0, h1, jac, pm,
):
    n_steps, width = mean_ref.shape
    units = w_in.shape[1]
    half = width // 2
    factor = math.sqrt(width + 1.0)
    mean = mean_ref[...]
    centre_pts = mean.astype(BF16)
    centre_f = centre_pts.astype(F32)
    base[...] = (jnp.dot(centre_pts, w_in[...], preferred_element_type=F32) + b_in[...]) * 0.5
    spread = spread_ref[...]
    up = (mean + factor * spread).astype(BF16).astype(F32)
    lo = (mean - factor * spread).astype(BF16).astype(F32)
    inv = 1.0 / (2.0 * factor * spread)
    for a, rows in enumerate((0.5 * (up - centre_f), 0.5 * (lo - centre_f), inv, (up - lo) * inv)):
        for k in range(n_steps):
            for b, block in enumerate(columns_of(rows[k : k + 1])):
                wide[a, k, pl.ds(b * LANES, LANES), :] = block

    def gelu(k, j0, dst):
        for c in range(0, units, 256):
            b = base[pl.ds(k, 1), pl.ds(c, 256)]
            for r in range(0, half, 16):
                w = w_in[pl.ds(j0 + r, 16), pl.ds(c, 256)].astype(F32)
                for s in range(2):
                    d = wide[s, k, pl.ds(j0 + r, 16), :]
                    y = b + jnp.concatenate([d, d], axis=1) * w
                    z = y * (y * y * (8.0 * C1) + 2.0 * C0)
                    dst[pl.ds(s * half + r, 16), pl.ds(c, 256)] = (y * jnp.tanh(z) + y).astype(BF16)

    def outer(k, j0, src):
        out = jnp.dot(src[...], w_out[...], preferred_element_type=F32)
        upper, lower = out[:half], out[half:]
        scale = wide[2, k, pl.ds(j0, half), :]
        own = wide[3, k, pl.ds(j0, half), :]
        keep = keep_ref[pl.ds(k, 1), :]
        rows = lax.broadcasted_iota(jnp.int32, (half, LANES), 0)
        lanes = lax.broadcasted_iota(jnp.int32, (half, LANES), 1)
        for c in range(0, width, LANES):
            v = (upper[:, c : c + LANES] - lower[:, c : c + LANES]) * scale
            if j0 <= c < j0 + half:
                v = v + jnp.where(rows == lanes + (c - j0), own, 0.0)
            jac[k, pl.ds(j0, half), pl.ds(c, LANES)] = v * keep[:, c : c + LANES]
        return jnp.sum(upper + lower, axis=0, keepdims=True)

    def step(k, carry):
        kp = jnp.maximum(k - 1, 0)
        total = outer(kp, half, h1)
        gelu(k, 0, h0)
        pm[pl.ds(kp, 1), :] = pm[pl.ds(kp, 1), :] + total
        total = outer(k, 0, h0)
        gelu(k, half, h1)
        pm[pl.ds(k, 1), :] = total
        return carry

    lax.fori_loop(0, n_steps, step, 0)
    pm[pl.ds(n_steps - 1, 1), :] = pm[pl.ds(n_steps - 1, 1), :] + outer(n_steps - 1, half, h1)

    points = 2.0 * width
    y = base[...]
    z = y * (y * y * (8.0 * C1) + 2.0 * C0)
    hidden = (y * jnp.tanh(z) + y).astype(BF16)
    centre = jnp.dot(hidden, w_out[...], preferred_element_type=F32) + b_out[...] + centre_f
    sums = pm[pl.ds(0, n_steps), :] + points * b_out[...] + ((points - 2.0) * centre_f + (up + lo))
    point_mean = centre / (width + 1.0) + sums / (2.0 * (width + 1.0))
    keep = keep_ref[...]
    free = keep * point_mean + (1.0 - keep) * obs_ref[...]
    consts = []
    for k in range(n_steps):
        moved = row_times(columns_of(mean[k : k + 1]), lambda r, c: jac[k, r, c])
        consts.append(free[k : k + 1] - moved)

    pad = jnp.zeros((7, width), F32)
    first = jac[0]
    pre[0] = first
    held = jnp.concatenate([first, consts[0], pad], axis=0)
    offsets[pl.ds(0, 1), :] = consts[0]
    for k in range(1, n_steps):
        held = product(held, jac[k])
        const = held[width : width + 1] + consts[k]
        offsets[pl.ds(k, 1), :] = const
        if k < n_steps - 1:
            pre[k] = held[:width]
            held = jnp.concatenate([held[:width], const, pad], axis=0)
        else:
            last[pl.ds(0, width), :] = held[:width]
            last[pl.ds(width, 8), :] = jnp.concatenate([const, pad], axis=0)


def pair_kernel(early, late, entry, chip, leaving):
    width = late.shape[1]
    both = product(early[...], late[pl.ds(0, width), :])
    chip[pl.ds(0, width), :] = both[:width]
    const = both[width : width + 1] + late[pl.ds(width, 1), :]
    chip[pl.ds(width, 8), :] = jnp.broadcast_to(const, (8, width))
    leaving[...] = row_times(columns_of(entry[...]), lambda r, c: chip[r, c]) + const


def hop_kernel(chip, entry, leaving):
    width = chip.shape[1]
    leaving[...] = row_times(columns_of(entry[...]), lambda r, c: chip[r, c]) + chip[pl.ds(width, 1), :]


def final_kernel(early, pre, last, offsets, entry, other, late_mask, out):
    n_steps, width = offsets.shape
    mid = row_times(columns_of(entry[...]), lambda r, c: early[r, c]) + early[pl.ds(width, 1), :]
    begin = jnp.where(late_mask[...] > 0.0, mid, other[...])
    cols = columns_of(begin)
    for k in range(n_steps):
        if k < n_steps - 1:
            moved = row_times(cols, lambda r, c: pre[k, r, c])
        else:
            moved = row_times(cols, lambda r, c: last[r, c])
        out[pl.ds(k, 1), :] = moved + offsets[pl.ds(k, 1), :]


def params():
    return pltpu.CompilerParams(vmem_limit_bytes=48 * 1024 * 1024)


def body(lin_mean, spread, keep, observed, start, w_in, b_in, w_out, b_out):
    n_steps, width = lin_mean.shape
    units = w_in.shape[1]
    size = lax.axis_size("tm")
    position = lax.axis_index("tm")
    shape = jax.ShapeDtypeStruct

    pre, last, offsets = pl.pallas_call(
        net_kernel,
        out_shape=(
            shape((n_steps - 1, width, width), F32),
            shape((width + 8, width), F32),
            shape((n_steps, width), F32),
        ),
        in_specs=[VMEM] * 8,
        out_specs=(VMEM,) * 3,
        scratch_shapes=[
            pltpu.VMEM((n_steps, units), F32),
            pltpu.VMEM((4, n_steps, width, LANES), F32),
            pltpu.VMEM((width, units), BF16),
            pltpu.VMEM((width, units), BF16),
            pltpu.VMEM((n_steps, width, width), F32),
            pltpu.VMEM((8, width), F32),
        ],
        compiler_params=params(),
    )(lin_mean, spread, keep, observed, w_in, b_in.reshape(1, units), w_out, b_out.reshape(1, width))

    swap = [(i, i ^ 1) for i in range(size)]
    early = lax.ppermute(last, "tm", swap)
    row = start.reshape(1, width)
    entry = jnp.where(position == 1, row, 0.0)
    chip, leaving = pl.pallas_call(
        pair_kernel,
        out_shape=(shape((width + 8, width), F32), shape((1, width), F32)),
        in_specs=[VMEM] * 3,
        out_specs=(VMEM,) * 2,
        compiler_params=params(),
    )(early, last, entry)
    for chip_at in range(1, size // 2):
        moved = lax.ppermute(leaving, "tm", [(2 * chip_at - 1, 2 * chip_at + 1)])
        entry = entry + moved
        if chip_at < size // 2 - 1:
            leaving = pl.pallas_call(
                hop_kernel,
                out_shape=shape((1, width), F32),
                in_specs=[VMEM] * 2,
                out_specs=VMEM,
                compiler_params=params(),
            )(chip, entry)
    other = lax.ppermute(entry, "tm", swap)
    late = jnp.broadcast_to((position % 2).astype(F32), (1, width))
    return pl.pallas_call(
        final_kernel,
        out_shape=shape((n_steps, width), F32),
        in_specs=[VMEM] * 7,
        out_specs=VMEM,
        compiler_params=params(),
    )(early, pre, last, offsets, entry, other, late)


def solution(mesh):
    rows = P(("groups", "tm"), None)
    placed = (rows, rows, rows, rows, P("groups"), P(), P(), P(), P())
    return jax.shard_map(body, mesh=mesh, in_specs=placed, out_specs=rows, check_vma=False)
```

time: 260 us -> 58.4 us (0.22)
  the two profiles are of different devices: /device:TPU:10 before, /device:TPU:27 now
where the time goes in v1:
time: 58.4 us; the launch traced here: 57.5 us
  Pallas kernels  22.6 us (39%)
  waiting for transfers between devices  18.9 us (32%)
  local copies, waits for them, and re-layouts  9.24 us (16%)
  starting transfers between devices  6.51 us (11%)
    pallas_call x1, Pallas kernels, body(): pl.pallas_call(net_kernel, out_shape=(shape((n_steps - 1, width, width),...  19.4 us
    ppermute x7, waiting for transfers between devices, body(): moved = lax.ppermute(leaving, 'tm', [(2 * chip_at - 1, 2 * chip_at + 1)])  15.4 us
    unnamed x20, local copies, waits for them, and re-layouts  9.24 us
    ppermute x7, starting transfers between devices, body(): moved = lax.ppermute(leaving, 'tm', [(2 * chip_at - 1, 2 * chip_at + 1)])  5.89 us
    ppermute x1, waiting for transfers between devices, body(): early = lax.ppermute(last, 'tm', swap)  2.3 us
    pallas_call x1, Pallas kernels, body(): pl.pallas_call(final_kernel, out_shape=shape((n_steps, width), F32), in_s...  1.33 us
  transfers between devices with their start and end apart: 9, of which 4 were waited for; matrix products, arithmetic and copies ran while one was open for 0% of the time, Pallas kernels for 0%

profile of v1, /device:TPU:27, one launch (start us, length us, event | category | flops | bytes accessed | tf_op | source)
XLA Modules:
  0.0 57.5 jit_solution(9974035575587293569)
XLA Ops:
  0.0 1.6 %copy-done.1 = bf16[512,2048]{1,0:T(8,128)(2,1)S(1)} copy-done((bf16[512,2048]{1,0:T(8,128)(2,1)S(1)}, bf16[512,2048]{1,0:T(8,128)(2,1)}, u32[]{:S(2)}) %copy-start.1) | copy-done | bytes 2097176
  1.6 1.6 %copy-done.2 = bf16[2048,512]{1,0:T(8,128)(2,1)S(1)} copy-done((bf16[2048,512]{1,0:T(8,128)(2,1)S(1)}, bf16[2048,512]{1,0:T(8,128)(2,1)}, u32[]{:S(2)}) %copy-start.2) | copy-done | bytes 2097176
  3.2 0.7 %copy-done.3 = f32[4,512]{1,0:T(4,128)S(1)} copy-done((f32[4,512]{1,0:T(4,128)S(1)}, f32[4,512]{1,0:T(4,128)}, u32[]{:S(2)}) %copy-start.3) | copy-done | bytes 8216
  3.9 0.7 %copy-done.4 = f32[4,512]{1,0:T(4,128)S(1)} copy-done((f32[4,512]{1,0:T(4,128)S(1)}, f32[4,512]{1,0:T(4,128)}, u32[]{:S(2)}) %copy-start.4) | copy-done | bytes 8216
  4.6 0.7 %copy-done.5 = f32[4,512]{1,0:T(4,128)S(1)} copy-done((f32[4,512]{1,0:T(4,128)S(1)}, f32[4,512]{1,0:T(4,128)}, u32[]{:S(2)}) %copy-start.5) | copy-done | bytes 8216
  5.3 0.7 %copy-done.6 = f32[4,512]{1,0:T(4,128)S(1)} copy-done((f32[4,512]{1,0:T(4,128)S(1)}, f32[4,512]{1,0:T(4,128)}, u32[]{:S(2)}) %copy-start.6) | copy-done | bytes 8216
  6.0 0.7 %copy-done.7 = f32[2048]{0:T(1024)S(1)} copy-done((f32[2048]{0:T(1024)S(1)}, f32[2048]{0:T(1024)}, u32[]{:S(2)}) %copy-start.7) | copy-done | bytes 8216
  6.7 0.7 %copy-done.8 = f32[512]{0:T(512)S(1)} copy-done((f32[512]{0:T(512)S(1)}, f32[512]{0:T(512)}, u32[]{:S(2)}) %copy-start.8) | copy-done | bytes 2072
  7.4 19.4 %shard_map.91 = (f32[3,512,512]{2,1,0:T(8,128)}, f32[520,512]{1,0:T(8,128)S(1)}, f32[4,512]{1,0:T(4,128)S(1)}) custom-call(f32[4,512]{1,0:T(4,128)S(1)} %copy-done.3, f32[4,512]{1,0:T(4,128)S(1)} %copy-done.4, f32[4,512]{1,0:T(4,128)S(1)} %copy-done.5, f32[4,512]{1,0:T(4,128)S(1)} %copy-done.6, bf16[512,2048]{1,0:T(8,128)(2,1)S(1)} %copy-done.1, ...), custom_call_target="tpu_custom_call" | custom-call | tf_op jit(solution)/shard_map/pallas_call | solution.py:187
  26.7 0.6 %collective-permute-start = (f32[520,512]{1,0:T(8,128)S(1)}, f32[520,512]{1,0:T(8,128)S(1)}, u32[]{:S(2)}, u32[]{:S(2)}) collective-permute-start(f32[520,512]{1,0:T(8,128)S(1)} %get-tuple-element.10.late.last), channel_id=1, source_target_pairs={{0,1},{1,0},{2,3},{3,2},{4,5},{5,4},{6,7},{7,6},{8,9},{9,8},{10,11... | collective-permute-start | bytes 3194888 | tf_op jit(solution)/shard_map/ppermute | solution.py:208
  27.3 2.3 %collective-permute-done.early = f32[520,512]{1,0:T(8,128)S(1)} collective-permute-done((f32[520,512]{1,0:T(8,128)S(1)}, f32[520,512]{1,0:T(8,128)S(1)}, u32[]{:S(2)}, u32[]{:S(2)}) %collective-permute-start) | collective-permute-done | bytes 1064992 | tf_op jit(solution)/shard_map/ppermute | solution.py:208
  29.6 1.0 %shard_map.92 = (f32[520,512]{1,0:T(8,128)S(1)}, f32[1,512]{1,0:T(1,128)S(1)}) custom-call(f32[520,512]{1,0:T(8,128)S(1)} %collective-permute-done.early, f32[520,512]{1,0:T(8,128)S(1)} %get-tuple-element.10.late.last, f32[1,512]{1,0:T(1,128)S(1)} %bitcast.3), custom_call_target="tpu_custom_call" | custom-call | tf_op jit(solution)/shard_map/pallas_call | solution.py:211
  30.7 0.7 %collective-permute-start.1 = (f32[1,512]{1,0:T(1,128)S(1)}, f32[1,512]{1,0:T(1,128)S(1)}, u32[]{:S(2)}, u32[]{:S(2)}) collective-permute-start(f32[1,512]{1,0:T(1,128)S(1)} %get-tuple-element.13), channel_id=1, source_target_pairs={{1,3},{17,19}} | collective-permute-start | bytes 6152 | tf_op jit(solution)/shard_map/ppermute | solution.py:219
  31.3 0.0 collective-permute-done.1
  31.4 0.1 shard_map.93
  31.5 0.7 %collective-permute-start.2 = (f32[1,512]{1,0:T(1,128)S(1)}, f32[1,512]{1,0:T(1,128)S(1)}, u32[]{:S(2)}, u32[]{:S(2)}) collective-permute-start(f32[1,512]{1,0:T(1,128)S(1)} %shard_map.93), channel_id=1, source_target_pairs={{3,5},{19,21}} | collective-permute-start | bytes 6152 | tf_op jit(solution)/shard_map/ppermute | solution.py:219
  32.2 0.1 shard_map.94
  32.3 0.7 %collective-permute-start.3 = (f32[1,512]{1,0:T(1,128)S(1)}, f32[1,512]{1,0:T(1,128)S(1)}, u32[]{:S(2)}, u32[]{:S(2)}) collective-permute-start(f32[1,512]{1,0:T(1,128)S(1)} %shard_map.94), channel_id=1, source_target_pairs={{5,7},{21,23}} | collective-permute-start | bytes 6152 | tf_op jit(solution)/shard_map/ppermute | solution.py:219
  33.0 0.1 shard_map.95
  33.2 0.7 %collective-permute-start.4 = (f32[1,512]{1,0:T(1,128)S(1)}, f32[1,512]{1,0:T(1,128)S(1)}, u32[]{:S(2)}, u32[]{:S(2)}) collective-permute-start(f32[1,512]{1,0:T(1,128)S(1)} %shard_map.95), channel_id=1, source_target_pairs={{7,9},{23,25}} | collective-permute-start | bytes 6152 | tf_op jit(solution)/shard_map/ppermute | solution.py:219
  33.9 0.0 collective-permute-done.4
  33.9 0.1 shard_map.96
  34.0 0.7 %collective-permute-start.5 = (f32[1,512]{1,0:T(1,128)S(1)}, f32[1,512]{1,0:T(1,128)S(1)}, u32[]{:S(2)}, u32[]{:S(2)}) collective-permute-start(f32[1,512]{1,0:T(1,128)S(1)} %shard_map.96), channel_id=1, source_target_pairs={{9,11},{25,27}} | collective-permute-start | bytes 6152 | tf_op jit(solution)/shard_map/ppermute | solution.py:219
  34.7 0.1 shard_map.97
  34.9 1.3 %collective-permute-start.6 = (f32[1,512]{1,0:T(1,128)S(1)}, f32[1,512]{1,0:T(1,128)S(1)}, u32[]{:S(2)}, u32[]{:S(2)}) collective-permute-start(f32[1,512]{1,0:T(1,128)S(1)} %shard_map.97), channel_id=1, source_target_pairs={{11,13},{27,29}} | collective-permute-start | bytes 6152 | tf_op jit(solution)/shard_map/ppermute | solution.py:219
  36.2 14.7 %collective-permute-done.6 = f32[1,512]{1,0:T(1,128)S(1)} collective-permute-done((f32[1,512]{1,0:T(1,128)S(1)}, f32[1,512]{1,0:T(1,128)S(1)}, u32[]{:S(2)}, u32[]{:S(2)}) %collective-permute-start.6) | collective-permute-done | bytes 2080 | tf_op jit(solution)/shard_map/ppermute | solution.py:219
  50.9 0.2 shard_map.98
  51.0 1.3 %collective-permute-start.7 = (f32[1,512]{1,0:T(1,128)S(1)}, f32[1,512]{1,0:T(1,128)S(1)}, u32[]{:S(2)}, u32[]{:S(2)}) collective-permute-start(f32[1,512]{1,0:T(1,128)S(1)} %shard_map.98), channel_id=1, source_target_pairs={{13,15},{29,31}} | collective-permute-start | bytes 6152 | tf_op jit(solution)/shard_map/ppermute | solution.py:219
  52.3 0.7 %collective-permute-done.7 = f32[1,512]{1,0:T(1,128)S(1)} collective-permute-done((f32[1,512]{1,0:T(1,128)S(1)}, f32[1,512]{1,0:T(1,128)S(1)}, u32[]{:S(2)}, u32[]{:S(2)}) %collective-permute-start.7) | collective-permute-done | bytes 2080 | tf_op jit(solution)/shard_map/ppermute | solution.py:219
  53.1 1.2 %collective-permute-done.8.other = f32[1,512]{1,0:T(1,128)S(1)} collective-permute-done((f32[1,512]{1,0:T(1,128)S(1)}, f32[1,512]{1,0:T(1,128)S(1)}, u32[]{:S(2)}, u32[]{:S(2)}) %collective-permute-start.8) | collective-permute-done | bytes 2080 | tf_op jit(solution)/shard_map/ppermute | solution.py:229
  54.2 1.9 %copy-done = f32[3,512,512]{2,1,0:T(8,128)S(1)} copy-done((f32[3,512,512]{2,1,0:T(8,128)S(1)}, f32[3,512,512]{2,1,0:T(8,128)}, u32[]{:S(2)}) %copy-start) | copy-done | bytes 3145752
  56.1 1.3 %shard_map.99 = f32[4,512]{1,0:T(4,128)} custom-call(f32[520,512]{1,0:T(8,128)S(1)} %collective-permute-done.early, f32[3,512,512]{2,1,0:T(8,128)S(1)} %copy-done, f32[520,512]{1,0:T(8,128)S(1)} %get-tuple-element.10.late.last, f32[4,512]{1,0:T(4,128)S(1)} %get-tuple-element.12.offsets, f32[1,512]{1,0:T(1,128)S(1)} %add.31.entry, ...), custom_call_target="tpu_custom_call" | custom-call | tf_op jit(solution)/shard_map/pallas_call | solution.py:231
  (24 shorter events, 0.1 us)
Async XLA Ops:
  0.0 1.6 %copy-start.1 = (bf16[512,2048]{1,0:T(8,128)(2,1)S(1)}, bf16[512,2048]{1,0:T(8,128)(2,1)}, u32[]{:S(2)}) copy-start(bf16[512,2048]{1,0:T(8,128)(2,1)} %w_in.1) | copy-start | bytes 6291460
  1.6 1.6 %copy-start.2 = (bf16[2048,512]{1,0:T(8,128)(2,1)S(1)}, bf16[2048,512]{1,0:T(8,128)(2,1)}, u32[]{:S(2)}) copy-start(bf16[2048,512]{1,0:T(8,128)(2,1)} %w_out.1) | copy-start | bytes 6291460
  3.2 0.7 %copy-start.3 = (f32[4,512]{1,0:T(4,128)S(1)}, f32[4,512]{1,0:T(4,128)}, u32[]{:S(2)}) copy-start(f32[4,512]{1,0:T(4,128)} %mean_ref.1) | copy-start | bytes 24580
  3.9 0.7 %copy-start.4 = (f32[4,512]{1,0:T(4,128)S(1)}, f32[4,512]{1,0:T(4,128)}, u32[]{:S(2)}) copy-start(f32[4,512]{1,0:T(4,128)} %spread_ref.1) | copy-start | bytes 24580
  4.6 0.7 %copy-start.5 = (f32[4,512]{1,0:T(4,128)S(1)}, f32[4,512]{1,0:T(4,128)}, u32[]{:S(2)}) copy-start(f32[4,512]{1,0:T(4,128)} %keep_ref.1) | copy-start | bytes 24580
  5.3 0.7 %copy-start.6 = (f32[4,512]{1,0:T(4,128)S(1)}, f32[4,512]{1,0:T(4,128)}, u32[]{:S(2)}) copy-start(f32[4,512]{1,0:T(4,128)} %obs_ref.1) | copy-start | bytes 24580
  6.0 0.7 %copy-start.7 = (f32[2048]{0:T(1024)S(1)}, f32[2048]{0:T(1024)}, u32[]{:S(2)}) copy-start(f32[2048]{0:T(1024)} %param.15) | copy-start | bytes 24580
  6.7 0.7 %copy-start.8 = (f32[512]{0:T(512)S(1)}, f32[512]{0:T(512)}, u32[]{:S(2)}) copy-start(f32[512]{0:T(512)} %param.17) | copy-start | bytes 6148
  7.4 20.0 %copy-start.9 = (f32[512]{0:T(512)S(1)}, f32[512]{0:T(512)}, u32[]{:S(2)}) copy-start(f32[512]{0:T(512)} %param.13) | copy-start | bytes 6148
  26.7 2.9 %collective-permute-start = (f32[520,512]{1,0:T(8,128)S(1)}, f32[520,512]{1,0:T(8,128)S(1)}, u32[]{:S(2)}, u32[]{:S(2)}) collective-permute-start(f32[520,512]{1,0:T(8,128)S(1)} %get-tuple-element.10.late.last), channel_id=1, source_target_pairs={{0,1},{1,0},{2,3},{3,2},{4,5},{5,4},{6,7},{7,6},{8,9},{9,8},{10,11... | collective-permute-start | bytes 3194888 | tf_op jit(solution)/shard_map/ppermute | solution.py:208
  30.7 0.7 %collective-permute-start.1 = (f32[1,512]{1,0:T(1,128)S(1)}, f32[1,512]{1,0:T(1,128)S(1)}, u32[]{:S(2)}, u32[]{:S(2)}) collective-permute-start(f32[1,512]{1,0:T(1,128)S(1)} %get-tuple-element.13), channel_id=1, source_target_pairs={{1,3},{17,19}} | collective-permute-start | bytes 6152 | tf_op jit(solution)/shard_map/ppermute | solution.py:219
  31.5 0.7 %collective-permute-start.2 = (f32[1,512]{1,0:T(1,128)S(1)}, f32[1,512]{1,0:T(1,128)S(1)}, u32[]{:S(2)}, u32[]{:S(2)}) collective-permute-start(f32[1,512]{1,0:T(1,128)S(1)} %shard_map.93), channel_id=1, source_target_pairs={{3,5},{19,21}} | collective-permute-start | bytes 6152 | tf_op jit(solution)/shard_map/ppermute | solution.py:219
  32.3 0.7 %collective-permute-start.3 = (f32[1,512]{1,0:T(1,128)S(1)}, f32[1,512]{1,0:T(1,128)S(1)}, u32[]{:S(2)}, u32[]{:S(2)}) collective-permute-start(f32[1,512]{1,0:T(1,128)S(1)} %shard_map.94), channel_id=1, source_target_pairs={{5,7},{21,23}} | collective-permute-start | bytes 6152 | tf_op jit(solution)/shard_map/ppermute | solution.py:219
  33.2 0.7 %collective-permute-start.4 = (f32[1,512]{1,0:T(1,128)S(1)}, f32[1,512]{1,0:T(1,128)S(1)}, u32[]{:S(2)}, u32[]{:S(2)}) collective-permute-start(f32[1,512]{1,0:T(1,128)S(1)} %shard_map.95), channel_id=1, source_target_pairs={{7,9},{23,25}} | collective-permute-start | bytes 6152 | tf_op jit(solution)/shard_map/ppermute | solution.py:219
  34.0 0.7 %collective-permute-start.5 = (f32[1,512]{1,0:T(1,128)S(1)}, f32[1,512]{1,0:T(1,128)S(1)}, u32[]{:S(2)}, u32[]{:S(2)}) collective-permute-start(f32[1,512]{1,0:T(1,128)S(1)} %shard_map.96), channel_id=1, source_target_pairs={{9,11},{25,27}} | collective-permute-start | bytes 6152 | tf_op jit(solution)/shard_map/ppermute | solution.py:219
  34.9 16.0 %collective-permute-start.6 = (f32[1,512]{1,0:T(1,128)S(1)}, f32[1,512]{1,0:T(1,128)S(1)}, u32[]{:S(2)}, u32[]{:S(2)}) collective-permute-start(f32[1,512]{1,0:T(1,128)S(1)} %shard_map.97), channel_id=1, source_target_pairs={{11,13},{27,29}} | collective-permute-start | bytes 6152 | tf_op jit(solution)/shard_map/ppermute | solution.py:219
  51.0 2.0 %collective-permute-start.7 = (f32[1,512]{1,0:T(1,128)S(1)}, f32[1,512]{1,0:T(1,128)S(1)}, u32[]{:S(2)}, u32[]{:S(2)}) collective-permute-start(f32[1,512]{1,0:T(1,128)S(1)} %shard_map.98), channel_id=1, source_target_pairs={{13,15},{29,31}} | collective-permute-start | bytes 6152 | tf_op jit(solution)/shard_map/ppermute | solution.py:219
  53.1 1.2 %collective-permute-start.8 = (f32[1,512]{1,0:T(1,128)S(1)}, f32[1,512]{1,0:T(1,128)S(1)}, u32[]{:S(2)}, u32[]{:S(2)}) collective-permute-start(f32[1,512]{1,0:T(1,128)S(1)} %add.31.entry), channel_id=1, source_target_pairs={{0,1},{1,0},{2,3},{3,2},{4,5},{5,4},{6,7},{7,6},{8,9},{9,8},{10,11... | collective-permute-start | bytes 6152 | tf_op jit(solution)/shard_map/ppermute | solution.py:229
  54.2 1.9 %copy-start = (f32[3,512,512]{2,1,0:T(8,128)S(1)}, f32[3,512,512]{2,1,0:T(8,128)}, u32[]{:S(2)}) copy-start(f32[3,512,512]{2,1,0:T(8,128)} %get-tuple-element.11.pre) | copy-start | bytes 9437188

commit v2 on v1

v2 whole, which is shorter than its diff:
```python
import functools
import math

import jax
import jax.numpy as jnp
from jax import lax
from jax.experimental import pallas as pl
from jax.experimental.pallas import tpu as pltpu
from jax.sharding import PartitionSpec as P

C0 = math.sqrt(2.0 / math.pi)
C1 = 0.044715 * C0
LANES = 128
F32 = jnp.float32
BF16 = jnp.bfloat16
VMEM = pl.BlockSpec(memory_space=pltpu.VMEM)
HBM = pl.BlockSpec(memory_space=pltpu.HBM)


def split(x):
    hi = x.astype(BF16)
    return hi, (x - hi.astype(F32)).astype(BF16)


def product(left, right):
    lhi, llo = split(left)
    rhi, rlo = split(right)
    return jnp.dot(
        jnp.concatenate([lhi, llo, lhi], axis=1),
        jnp.concatenate([rhi, rhi, rlo], axis=0),
        preferred_element_type=F32,
    )


def columns_of(row):
    width = row.shape[1]
    return [
        jnp.transpose(jnp.broadcast_to(row[:, b : b + LANES], (LANES, LANES)))
        for b in range(0, width, LANES)
    ]


def row_times(cols, matrix):
    width = len(cols) * LANES
    parts = []
    for c in range(0, width, LANES):
        total = None
        for b in range(len(cols)):
            term = jnp.sum(
                (cols[b] * matrix(pl.ds(b * LANES, LANES), pl.ds(c, LANES))).reshape(LANES // 8, 8, LANES),
                axis=0,
            )
            total = term if total is None else total + term
        parts.append(jnp.sum(total, axis=0, keepdims=True))
    return jnp.concatenate(parts, axis=1)


def net_kernel(
    mean_h, spread_h, keep_h, obs_h, b_in_h, b_out_h, w_in_h, w_out_h,
    pre, last, offsets,
    mean_ref, spread_ref, keep_ref, obs_ref, b_in, b_out, w_in, w_out,
    turned, w_wide, base, wide, h0, h1, jac, pm, held_ref, sems, out_sems,
):
    n_steps, width = mean_ref.shape
    units = w_in.shape[1]
    half = width // 2
    factor = math.sqrt(width + 1.0)
    sources = (mean_h, spread_h, keep_h, obs_h, b_in_h, b_out_h)
    targets = (mean_ref, spread_ref, keep_ref, obs_ref, b_in, b_out)
    copies = [
        pltpu.make_async_copy(source, target, sems.at[i])
        for i, (source, target) in enumerate(zip(sources, targets))
    ]
    quarter = units // 4
    for i in range(4):
        part = pl.ds(i * quarter, quarter)
        copies.append(pltpu.make_async_copy(w_in_h.at[:, part], w_in.at[:, part], sems.at[6 + i]))
    copies.append(pltpu.make_async_copy(w_out_h, w_out, sems.at[10]))
    for copy in copies:
        copy.start()
    for copy in copies[:6]:
        copy.wait()

    mean = mean_ref[...]
    centre_pts = mean.astype(BF16)
    centre_f = centre_pts.astype(F32)
    spread = spread_ref[...]
    up = (mean + factor * spread).astype(BF16).astype(F32)
    lo = (mean - factor * spread).astype(BF16).astype(F32)
    inv = 1.0 / (2.0 * factor * spread)
    eye = lax.broadcasted_iota(jnp.int32, (LANES, LANES), 0) == lax.broadcasted_iota(
        jnp.int32, (LANES, LANES), 1
    )
    kinds = (0.5 * (up - centre_f), 0.5 * (lo - centre_f), inv, (up - lo) * inv)
    stacked = jnp.concatenate(kinds + (jnp.zeros((LANES - 4 * n_steps, width), F32),), axis=0)
    for b in range(0, width, LANES):
        turned[pl.ds(b, LANES), :] = jnp.transpose(stacked[:, b : b + LANES])

    def widen(k):
        for b in range(0, width, LANES):
            for a in range(4):
                at = a * n_steps + k
                block = jnp.broadcast_to(turned[pl.ds(b, LANES), at : at + 1], (LANES, LANES))
                if a == 3:
                    block = jnp.where(eye, block, 0.0)
                wide[a, k, pl.ds(b, LANES), :] = block

    widen(0)

    def gelu(k, j0, dst):
        for c in range(0, units, 256):
            if k == 0 and j0 == 0 and c % quarter == 0:
                copies[6 + c // quarter].wait()
                part = pl.ds(c, quarter)
                base[:, part] = (
                    jnp.dot(centre_pts, w_in[:, part], preferred_element_type=F32) + b_in[:, part]
                ) * 0.5
            b = base[pl.ds(k, 1), pl.ds(c, 256)]
            for r in range(0, half, 16):
                place = (pl.ds(j0 + r, 16), pl.ds(c, 256))
                if k == 0:
                    w = w_in[place].astype(F32)
                    w_wide[place] = w
                else:
                    w = w_wide[place]
                for s in range(2):
                    d = wide[s, k, pl.ds(j0 + r, 16), :]
                    y = b + jnp.concatenate([d, d], axis=1) * w
                    z = y * (y * y * (8.0 * C1) + 2.0 * C0)
                    dst[pl.ds(s * half + r, 16), pl.ds(c, 256)] = (y * jnp.tanh(z) + y).astype(BF16)

    def outer(k, j0, src):
        out = jnp.dot(src[...], w_out[...], preferred_element_type=F32)
        keep = keep_ref[pl.ds(k, 1), :]
        sums = []
        for c in range(0, width, LANES):
            upper, lower = out[:half, c : c + LANES], out[half:, c : c + LANES]
            for r in range(0, half, LANES):
                v = (upper[r : r + LANES] - lower[r : r + LANES]) * wide[2, k, pl.ds(j0 + r, LANES), :]
                if c == j0 + r:
                    v = v + wide[3, k, pl.ds(c, LANES), :]
                jac[k, pl.ds(j0 + r, LANES), pl.ds(c, LANES)] = v * keep[:, c : c + LANES]
            sums.append(jnp.sum(upper + lower, axis=0, keepdims=True))
        return jnp.concatenate(sums, axis=1)

    sends = []

    def compose(k):
        held = product(held_ref[k - 1] if k > 1 else jac[0], jac[k])
        if k < n_steps - 1:
            held_ref[k] = held
        else:
            last[pl.ds(0, width), :] = held
        if k < n_steps - 1:
            sends.append(pltpu.make_async_copy(held_ref.at[k], pre.at[k], out_sems.at[k]))
            sends[-1].start()

    slots = (h0, h1)
    tiles = 2 * n_steps
    for tile in range(tiles + 1):
        if tile < tiles:
            gelu(tile // 2, (tile % 2) * half, slots[tile % 2])
        if tile % 2 == 0 and tile + 2 < tiles:
            widen(tile // 2 + 1)
        if tile == 0:
            copies[10].wait()
        if tile > 0:
            k, side = (tile - 1) // 2, (tile - 1) % 2
            total = outer(k, side * half, slots[side])
            pm[pl.ds(k, 1), :] = total if side == 0 else pm[pl.ds(k, 1), :] + total
        if tile == 3:
            sends.append(pltpu.make_async_copy(jac.at[0], pre.at[0], out_sems.at[0]))
            sends[-1].start()
        if tile >= 5 and tile % 2 == 1:
            compose((tile - 3) // 2)

    points = 2.0 * width
    y = base[...]
    z = y * (y * y * (8.0 * C1) + 2.0 * C0)
    hidden = (y * jnp.tanh(z) + y).astype(BF16)
    centre = jnp.dot(hidden, w_out[...], preferred_element_type=F32) + b_out[...] + centre_f
    sums = pm[pl.ds(0, n_steps), :] + points * b_out[...] + ((points - 2.0) * centre_f + (up + lo))
    point_mean = centre / (width + 1.0) + sums / (2.0 * (width + 1.0))
    keep = keep_ref[...]
    free = keep * point_mean + (1.0 - keep) * obs_ref[...]
    consts = []
    for k in range(n_steps):
        moved = row_times(columns_of(mean[k : k + 1]), lambda r, c: jac[k, r, c])
        consts.append(free[k : k + 1] - moved)

    for k in range((tiles - 3) // 2 + 1, n_steps):
        compose(k)
    const = consts[0]
    offsets[pl.ds(0, 1), :] = const
    for k in range(1, n_steps):
        const = row_times(columns_of(const), lambda r, c: jac[k, r, c]) + consts[k]
        offsets[pl.ds(k, 1), :] = const
    last[pl.ds(width, 8), :] = jnp.concatenate([const, jnp.zeros((7, width), F32)], axis=0)
    for send in sends:
        send.wait()


def fetch_kernel(source, target, sem):
    copy = pltpu.make_async_copy(source, target, sem)
    copy.start()
    copy.wait()


def first_kernel(early, late, entry, leaving):
    width = late.shape[1]
    mid = row_times(columns_of(entry[...]), lambda r, c: early[r, c]) + early[pl.ds(width, 1), :]
    leaving[...] = row_times(columns_of(mid), lambda r, c: late[r, c]) + late[pl.ds(width, 1), :]


def pair_kernel(early, late, chip):
    width = late.shape[1]
    both = product(early[...], late[pl.ds(0, width), :])
    chip[pl.ds(0, width), :] = both[:width]
    const = both[width : width + 1] + late[pl.ds(width, 1), :]
    chip[pl.ds(width, 8), :] = jnp.broadcast_to(const, (8, width))


def hop_kernel(chip, entry, leaving):
    width = chip.shape[1]
    leaving[...] = row_times(columns_of(entry[...]), lambda r, c: chip[r, c]) + chip[pl.ds(width, 1), :]


def final_kernel(early, pre_h, last, offsets_h, entry, other, late_mask, out, pre, offsets, sems):
    n_steps, width = offsets.shape
    gets = [pltpu.make_async_copy(pre_h.at[k], pre.at[k], sems.at[k]) for k in range(n_steps - 1)]
    gets.append(pltpu.make_async_copy(offsets_h, offsets, sems.at[n_steps - 1]))
    for get in gets:
        get.start()
    mid = row_times(columns_of(entry[...]), lambda r, c: early[r, c]) + early[pl.ds(width, 1), :]
    begin = jnp.where(late_mask[...] > 0.0, mid, other[...])
    cols = columns_of(begin)
    gets[n_steps - 1].wait()
    for k in range(n_steps):
        if k < n_steps - 1:
            gets[k].wait()
            moved = row_times(cols, lambda r, c: pre[k, r, c])
        else:
            moved = row_times(cols, lambda r, c: last[r, c])
        out[pl.ds(k, 1), :] = moved + offsets[pl.ds(k, 1), :]


def params(mib):
    return pltpu.CompilerParams(vmem_limit_bytes=mib * 1024 * 1024)


def body(lin_mean, spread, keep, observed, start, w_in, b_in, w_out, b_out):
    n_steps, width = lin_mean.shape
    units = w_in.shape[1]
    size = lax.axis_size("tm")
    position = lax.axis_index("tm")
    shape = jax.ShapeDtypeStruct

    small = pltpu.VMEM((n_steps, width), F32)
    pre, last, offsets = pl.pallas_call(
        net_kernel,
        out_shape=(
            shape((n_steps - 1, width, width), F32),
            shape((width + 8, width), F32),
            shape((n_steps, width), F32),
        ),
        in_specs=[HBM] * 8,
        out_specs=(HBM, VMEM, VMEM),
        scratch_shapes=[
            small, small, small, small,
            pltpu.VMEM((1, units), F32),
            pltpu.VMEM((1, width), F32),
            pltpu.VMEM((width, units), BF16),
            pltpu.VMEM((units, width), BF16),
            pltpu.VMEM((width, LANES), F32),
            pltpu.VMEM((width, units), F32),
            pltpu.VMEM((n_steps, units), F32),
            pltpu.VMEM((4, n_steps, width, LANES), F32),
            pltpu.VMEM((width, units), BF16),
            pltpu.VMEM((width, units), BF16),
            pltpu.VMEM((n_steps, width, width), F32),
            pltpu.VMEM((8, width), F32),
            pltpu.VMEM((n_steps - 1, width, width), F32),
            pltpu.SemaphoreType.DMA((11,)),
            pltpu.SemaphoreType.DMA((n_steps,)),
        ],
        compiler_params=params(60),
    )(lin_mean, spread, keep, observed, b_in.reshape(1, units), b_out.reshape(1, width), w_in, w_out)

    swap = [(i, i ^ 1) for i in range(size)]
    row = start.reshape(1, width)
    early = lax.ppermute(last, "tm", swap)
    late = pl.pallas_call(
        fetch_kernel,
        out_shape=shape((width + 8, width), F32),
        in_specs=[HBM],
        out_specs=VMEM,
        scratch_shapes=[pltpu.SemaphoreType.DMA],
        compiler_params=params(16),
    )(last)
    leaving = pl.pallas_call(
        first_kernel,
        out_shape=shape((1, width), F32),
        in_specs=[VMEM] * 3,
        out_specs=VMEM,
        compiler_params=params(16),
    )(early, late, row)
    chip = pl.pallas_call(
        pair_kernel,
        out_shape=shape((width + 8, width), F32),
        in_specs=[VMEM] * 2,
        out_specs=VMEM,
        compiler_params=params(16),
    )(early, late)
    entry = row
    for chip_at in range(1, size // 2):
        if chip_at % 2 == 1 and size % 4 == 0:
            moved = lax.ppermute(leaving, "tm", [(i, i ^ 2) for i in range(size)])
        else:
            moved = lax.ppermute(leaving, "tm", [(2 * chip_at - 1, 2 * chip_at + 1)])
        entry = jnp.where(position == 2 * chip_at + 1, moved, entry)
        if chip_at < size // 2 - 1:
            leaving = pl.pallas_call(
                hop_kernel,
                out_shape=shape((1, width), F32),
                in_specs=[VMEM] * 2,
                out_specs=VMEM,
                compiler_params=params(16),
            )(chip, entry)
    other = lax.ppermute(entry, "tm", swap)
    late_mask = jnp.broadcast_to((position % 2).astype(F32), (1, width))
    return pl.pallas_call(
        final_kernel,
        out_shape=shape((n_steps, width), F32),
        in_specs=[VMEM, HBM, VMEM, HBM] + [VMEM] * 3,
        out_specs=VMEM,
        scratch_shapes=[
            pltpu.VMEM((n_steps - 1, width, width), F32),
            pltpu.VMEM((n_steps, width), F32),
            pltpu.SemaphoreType.DMA((n_steps,)),
        ],
        compiler_params=params(50),
    )(early, pre, late, offsets, entry, other, late_mask)


def solution(mesh):
    rows = P(("groups", "tm"), None)
    placed = (rows, rows, rows, rows, P("groups"), P(), P(), P(), P())
    return jax.shard_map(body, mesh=mesh, in_specs=placed, out_specs=rows, check_vma=False)
```

time: 58.4 us -> 47.6 us (0.82); the launches traced: 57.5 us -> 47.4 us
  local copies, waits for them, and re-layouts: 9.24 us -> 1.24 us
  waiting for transfers between devices: 18.9 us -> 14.1 us
  Pallas kernels: 22.6 us -> 24.3 us
  starting transfers between devices: 6.51 us -> 7.34 us
    ppermute x7 -> x3, waiting for transfers between devices: 15.4 us -> 6.84 us  [body(): moved = lax.ppermute(leaving, 'tm', [(2 * chip_at - 1, 2 * chip_at + 1)])]
    unnamed x20 -> x6, local copies, waits for them, and re-layouts: 9.24 us -> 1.24 us
    ppermute x0 -> x4, waiting for transfers between devices: none -> 4.99 us  [body(): moved = lax.ppermute(leaving, 'tm', [(i, i ^ 2) for i in range(size)])]
    ppermute x0 -> x4, starting transfers between devices: none -> 3.98 us  [body(): moved = lax.ppermute(leaving, 'tm', [(i, i ^ 2) for i in range(size)])]
    ppermute x7 -> x3, starting transfers between devices: 5.89 us -> 2.62 us  [body(): moved = lax.ppermute(leaving, 'tm', [(2 * chip_at - 1, 2 * chip_at + 1)])]
    pallas_call x1, Pallas kernels: 1.33 us -> 2.75 us  [body(): pl.pallas_call(final_kernel, out_shape=shape((n_steps, width), F32), in_s...]
    ppermute x1, waiting for transfers between devices: 2.3 us -> 1.18 us  [body(): early = lax.ppermute(last, 'tm', swap)]
    pallas_call x1 -> x3, Pallas kernels: 1.02 us -> 1.4 us  [the longest x1 1.01 us: body(): pl.pallas_call(pair_kernel, out_shape=shape((width + 8, width), F32), in_...]
  transfers between devices with their start and end apart: 9 -> 9, of which waited for: 4 -> 7; matrix products, arithmetic and copies ran while one was open for 0% -> 0% of each run, Pallas kernels for 0% -> 2%
where the time goes in v2:
time: 47.6 us; the launch traced here: 47.4 us
  Pallas kernels  24.3 us (51%)
  waiting for transfers between devices  14.1 us (30%)
  starting transfers between devices  7.34 us (15%)
  local copies, waits for them, and re-layouts  1.24 us (3%)
    pallas_call x1, Pallas kernels, body(): pl.pallas_call(net_kernel, out_shape=(shape((n_steps - 1, width, width),...  19.3 us
    ppermute x3, waiting for transfers between devices, body(): moved = lax.ppermute(leaving, 'tm', [(2 * chip_at - 1, 2 * chip_at + 1)])  6.84 us
    ppermute x4, waiting for transfers between devices, body(): moved = lax.ppermute(leaving, 'tm', [(i, i ^ 2) for i in range(size)])  4.99 us
    ppermute x4, starting transfers between devices, body(): moved = lax.ppermute(leaving, 'tm', [(i, i ^ 2) for i in range(size)])  3.98 us
    pallas_call x1, Pallas kernels, body(): pl.pallas_call(final_kernel, out_shape=shape((n_steps, width), F32), in_s...  2.75 us
    ppermute x3, starting transfers between devices, body(): moved = lax.ppermute(leaving, 'tm', [(2 * chip_at - 1, 2 * chip_at + 1)])  2.62 us
    unnamed x6, local copies, waits for them, and re-layouts  1.24 us
    ppermute x1, waiting for transfers between devices, body(): early = lax.ppermute(last, 'tm', swap)  1.18 us
  transfers between devices with their start and end apart: 9, of which 7 were waited for; matrix products, arithmetic and copies ran while one was open for 0% of the time, Pallas kernels for 2%

profile of v2, /device:TPU:27, one launch (start us, length us, event | category | flops | bytes accessed | tf_op | source)
XLA Modules:
  0.0 47.4 jit_solution(5452528652097938084)
XLA Ops:
  0.0 19.3 %shard_map.91 = (f32[3,512,512]{2,1,0:T(8,128)}, f32[520,512]{1,0:T(8,128)}, f32[4,512]{1,0:T(4,128)}) custom-call(f32[4,512]{1,0:T(4,128)} %mean_h.1, f32[4,512]{1,0:T(4,128)} %spread_h.1, f32[4,512]{1,0:T(4,128)} %keep_h.1, f32[4,512]{1,0:T(4,128)} %obs_h.1, f32[1,2048]{1,0:T(1,128)} %bitcast.5, f32[1,512]{1,0:T(1,128)} %bitcast.6, ...), custom_call_target="tpu_custom_call" | custom-call | tf_op jit(solution)/shard_map/pallas_call | solution.py:259
  19.3 0.7 %collective-permute-start = (f32[520,512]{1,0:T(8,128)}, f32[520,512]{1,0:T(8,128)S(1)}, u32[]{:S(2)}, u32[]{:S(2)}) collective-permute-start(f32[520,512]{1,0:T(8,128)} %get-tuple-element.8.source), channel_id=1, source_target_pairs={{0,1},{1,0},{2,3},{3,2},{4,5},{5,4},{6,7},{7,6},{8,9},{9,8},{10,11... | collective-permute-start | bytes 3194888 | tf_op jit(solution)/shard_map/ppermute | solution.py:291
  20.0 1.2 %copy-done = f32[520,512]{1,0:T(8,128)S(1)} copy-done((f32[520,512]{1,0:T(8,128)S(1)}, f32[520,512]{1,0:T(8,128)}, u32[]{:S(2)}) %copy-start) | copy-done | bytes 1064984
  21.3 0.1 shard_map.92.late.last
  21.4 1.2 %collective-permute-done.early = f32[520,512]{1,0:T(8,128)S(1)} collective-permute-done((f32[520,512]{1,0:T(8,128)}, f32[520,512]{1,0:T(8,128)S(1)}, u32[]{:S(2)}, u32[]{:S(2)}) %collective-permute-start) | collective-permute-done | bytes 1064992 | tf_op jit(solution)/shard_map/ppermute | solution.py:291
  22.5 0.0 copy-done.2
  22.5 0.3 shard_map.94
  22.8 1.3 %collective-permute-start.1 = (f32[1,512]{1,0:T(1,128)S(1)}, f32[1,512]{1,0:T(1,128)S(1)}, u32[]{:S(2)}, u32[]{:S(2)}) collective-permute-start(f32[1,512]{1,0:T(1,128)S(1)} %shard_map.94), channel_id=1, source_target_pairs={{0,2},{1,3},{2,0},{3,1},{4,6},{5,7},{6,4},{7,5},{8,10},{9,11},{10,... | collective-permute-start | bytes 6152 | tf_op jit(solution)/shard_map/ppermute | solution.py:317
  24.1 1.0 %shard_map.93.chip = f32[520,512]{1,0:T(8,128)S(1)} custom-call(f32[520,512]{1,0:T(8,128)S(1)} %collective-permute-done.early, f32[520,512]{1,0:T(8,128)S(1)} %shard_map.92.late.last), custom_call_target="tpu_custom_call" | custom-call | tf_op jit(solution)/shard_map/pallas_call | solution.py:307
  25.2 0.2 collective-permute-done.1
  25.3 0.2 shard_map.95
  25.5 0.7 %collective-permute-start.2 = (f32[1,512]{1,0:T(1,128)S(1)}, f32[1,512]{1,0:T(1,128)S(1)}, u32[]{:S(2)}, u32[]{:S(2)}) collective-permute-start(f32[1,512]{1,0:T(1,128)S(1)} %shard_map.95), channel_id=1, source_target_pairs={{3,5},{19,21}} | collective-permute-start | bytes 6152 | tf_op jit(solution)/shard_map/ppermute | solution.py:319
  26.2 0.0 collective-permute-done.2
  26.2 0.1 shard_map.96
  26.3 1.3 %collective-permute-start.3 = (f32[1,512]{1,0:T(1,128)S(1)}, f32[1,512]{1,0:T(1,128)S(1)}, u32[]{:S(2)}, u32[]{:S(2)}) collective-permute-start(f32[1,512]{1,0:T(1,128)S(1)} %shard_map.96), channel_id=1, source_target_pairs={{0,2},{1,3},{2,0},{3,1},{4,6},{5,7},{6,4},{7,5},{8,10},{9,11},{10,... | collective-permute-start | bytes 6152 | tf_op jit(solution)/shard_map/ppermute | solution.py:317
  27.7 1.2 %collective-permute-done.3 = f32[1,512]{1,0:T(1,128)S(1)} collective-permute-done((f32[1,512]{1,0:T(1,128)S(1)}, f32[1,512]{1,0:T(1,128)S(1)}, u32[]{:S(2)}, u32[]{:S(2)}) %collective-permute-start.3) | collective-permute-done | bytes 2080 | tf_op jit(solution)/shard_map/ppermute | solution.py:317
  28.9 0.2 shard_map.97
  29.0 0.7 %collective-permute-start.4 = (f32[1,512]{1,0:T(1,128)S(1)}, f32[1,512]{1,0:T(1,128)S(1)}, u32[]{:S(2)}, u32[]{:S(2)}) collective-permute-start(f32[1,512]{1,0:T(1,128)S(1)} %shard_map.97), channel_id=1, source_target_pairs={{7,9},{23,25}} | collective-permute-start | bytes 6152 | tf_op jit(solution)/shard_map/ppermute | solution.py:319
  29.7 0.0 collective-permute-done.4
  29.7 0.1 shard_map.98
  29.9 1.3 %collective-permute-start.5 = (f32[1,512]{1,0:T(1,128)S(1)}, f32[1,512]{1,0:T(1,128)S(1)}, u32[]{:S(2)}, u32[]{:S(2)}) collective-permute-start(f32[1,512]{1,0:T(1,128)S(1)} %shard_map.98), channel_id=1, source_target_pairs={{0,2},{1,3},{2,0},{3,1},{4,6},{5,7},{6,4},{7,5},{8,10},{9,11},{10,... | collective-permute-start | bytes 6152 | tf_op jit(solution)/shard_map/ppermute | solution.py:317
  31.2 1.2 %collective-permute-done.5 = f32[1,512]{1,0:T(1,128)S(1)} collective-permute-done((f32[1,512]{1,0:T(1,128)S(1)}, f32[1,512]{1,0:T(1,128)S(1)}, u32[]{:S(2)}, u32[]{:S(2)}) %collective-permute-start.5) | collective-permute-done | bytes 2080 | tf_op jit(solution)/shard_map/ppermute | solution.py:317
  32.4 0.1 shard_map.99
  32.5 1.3 %collective-permute-start.6 = (f32[1,512]{1,0:T(1,128)S(1)}, f32[1,512]{1,0:T(1,128)S(1)}, u32[]{:S(2)}, u32[]{:S(2)}) collective-permute-start(f32[1,512]{1,0:T(1,128)S(1)} %shard_map.99), channel_id=1, source_target_pairs={{11,13},{27,29}} | collective-permute-start | bytes 6152 | tf_op jit(solution)/shard_map/ppermute | solution.py:319
  33.8 6.8 %collective-permute-done.6 = f32[1,512]{1,0:T(1,128)S(1)} collective-permute-done((f32[1,512]{1,0:T(1,128)S(1)}, f32[1,512]{1,0:T(1,128)S(1)}, u32[]{:S(2)}, u32[]{:S(2)}) %collective-permute-start.6) | collective-permute-done | bytes 2080 | tf_op jit(solution)/shard_map/ppermute | solution.py:319
  40.7 0.1 shard_map.100
  40.8 0.1 collective-permute-start.7
  40.9 2.4 %collective-permute-done.7 = f32[1,512]{1,0:T(1,128)S(1)} collective-permute-done((f32[1,512]{1,0:T(1,128)S(1)}, f32[1,512]{1,0:T(1,128)S(1)}, u32[]{:S(2)}, u32[]{:S(2)}) %collective-permute-start.7) | collective-permute-done | bytes 2080 | tf_op jit(solution)/shard_map/ppermute | solution.py:317
  43.3 0.0 collective-permute-start.8
  43.3 1.1 %collective-permute-done.8.other = f32[1,512]{1,0:T(1,128)S(1)} collective-permute-done((f32[1,512]{1,0:T(1,128)S(1)}, f32[1,512]{1,0:T(1,128)S(1)}, u32[]{:S(2)}, u32[]{:S(2)}) %collective-permute-start.8) | collective-permute-done | bytes 2080 | tf_op jit(solution)/shard_map/ppermute | solution.py:329
  44.5 0.0 copy-done.1
  44.5 2.7 %shard_map.101 = f32[4,512]{1,0:T(4,128)} custom-call(f32[520,512]{1,0:T(8,128)S(1)} %collective-permute-done.early, f32[3,512,512]{2,1,0:T(8,128)} %get-tuple-element.9.pre_h, f32[520,512]{1,0:T(8,128)S(1)} %shard_map.92.late.last, f32[4,512]{1,0:T(4,128)S(1)} %copy-done.1, f32[1,512]{1,0:T(1,128)S(1)} %broadcast_select_fusion.6.entry, ...), custom_call_target="tpu_custom_call" | custom-call | tf_op jit(solution)/shard_map/pallas_call | solution.py:331
  (11 shorter events, 0.0 us)
Async XLA Ops:
  19.3 3.3 %collective-permute-start = (f32[520,512]{1,0:T(8,128)}, f32[520,512]{1,0:T(8,128)S(1)}, u32[]{:S(2)}, u32[]{:S(2)}) collective-permute-start(f32[520,512]{1,0:T(8,128)} %get-tuple-element.8.source), channel_id=1, source_target_pairs={{0,1},{1,0},{2,3},{3,2},{4,5},{5,4},{6,7},{7,6},{8,9},{9,8},{10,11... | collective-permute-start | bytes 3194888 | tf_op jit(solution)/shard_map/ppermute | solution.py:291
  20.0 1.2 %copy-start = (f32[520,512]{1,0:T(8,128)S(1)}, f32[520,512]{1,0:T(8,128)}, u32[]{:S(2)}) copy-start(f32[520,512]{1,0:T(8,128)} %get-tuple-element.8.source) | copy-start | bytes 3194884
  21.2 1.3 %copy-start.2 = (f32[512]{0:T(512)S(1)}, f32[512]{0:T(512)}, u32[]{:S(2)}) copy-start(f32[512]{0:T(512)} %param.13) | copy-start | bytes 6148
  22.8 2.5 %collective-permute-start.1 = (f32[1,512]{1,0:T(1,128)S(1)}, f32[1,512]{1,0:T(1,128)S(1)}, u32[]{:S(2)}, u32[]{:S(2)}) collective-permute-start(f32[1,512]{1,0:T(1,128)S(1)} %shard_map.94), channel_id=1, source_target_pairs={{0,2},{1,3},{2,0},{3,1},{4,6},{5,7},{6,4},{7,5},{8,10},{9,11},{10,... | collective-permute-start | bytes 6152 | tf_op jit(solution)/shard_map/ppermute | solution.py:317
  25.5 0.7 %collective-permute-start.2 = (f32[1,512]{1,0:T(1,128)S(1)}, f32[1,512]{1,0:T(1,128)S(1)}, u32[]{:S(2)}, u32[]{:S(2)}) collective-permute-start(f32[1,512]{1,0:T(1,128)S(1)} %shard_map.95), channel_id=1, source_target_pairs={{3,5},{19,21}} | collective-permute-start | bytes 6152 | tf_op jit(solution)/shard_map/ppermute | solution.py:319
  26.3 2.5 %collective-permute-start.3 = (f32[1,512]{1,0:T(1,128)S(1)}, f32[1,512]{1,0:T(1,128)S(1)}, u32[]{:S(2)}, u32[]{:S(2)}) collective-permute-start(f32[1,512]{1,0:T(1,128)S(1)} %shard_map.96), channel_id=1, source_target_pairs={{0,2},{1,3},{2,0},{3,1},{4,6},{5,7},{6,4},{7,5},{8,10},{9,11},{10,... | collective-permute-start | bytes 6152 | tf_op jit(solution)/shard_map/ppermute | solution.py:317
  29.0 0.7 %collective-permute-start.4 = (f32[1,512]{1,0:T(1,128)S(1)}, f32[1,512]{1,0:T(1,128)S(1)}, u32[]{:S(2)}, u32[]{:S(2)}) collective-permute-start(f32[1,512]{1,0:T(1,128)S(1)} %shard_map.97), channel_id=1, source_target_pairs={{7,9},{23,25}} | collective-permute-start | bytes 6152 | tf_op jit(solution)/shard_map/ppermute | solution.py:319
  29.9 2.5 %collective-permute-start.5 = (f32[1,512]{1,0:T(1,128)S(1)}, f32[1,512]{1,0:T(1,128)S(1)}, u32[]{:S(2)}, u32[]{:S(2)}) collective-permute-start(f32[1,512]{1,0:T(1,128)S(1)} %shard_map.98), channel_id=1, source_target_pairs={{0,2},{1,3},{2,0},{3,1},{4,6},{5,7},{6,4},{7,5},{8,10},{9,11},{10,... | collective-permute-start | bytes 6152 | tf_op jit(solution)/shard_map/ppermute | solution.py:317
  32.4 12.1 %copy-start.1 = (f32[4,512]{1,0:T(4,128)S(1)}, f32[4,512]{1,0:T(4,128)}, u32[]{:S(2)}) copy-start(f32[4,512]{1,0:T(4,128)} %get-tuple-element.10.offsets_h) | copy-start | bytes 24580
  32.5 8.1 %collective-permute-start.6 = (f32[1,512]{1,0:T(1,128)S(1)}, f32[1,512]{1,0:T(1,128)S(1)}, u32[]{:S(2)}, u32[]{:S(2)}) collective-permute-start(f32[1,512]{1,0:T(1,128)S(1)} %shard_map.99), channel_id=1, source_target_pairs={{11,13},{27,29}} | collective-permute-start | bytes 6152 | tf_op jit(solution)/shard_map/ppermute | solution.py:319
  40.8 2.5 %collective-permute-start.7 = (f32[1,512]{1,0:T(1,128)S(1)}, f32[1,512]{1,0:T(1,128)S(1)}, u32[]{:S(2)}, u32[]{:S(2)}) collective-permute-start(f32[1,512]{1,0:T(1,128)S(1)} %shard_map.100), channel_id=1, source_target_pairs={{0,2},{1,3},{2,0},{3,1},{4,6},{5,7},{6,4},{7,5},{8,10},{9,11},{10,... | collective-permute-start | bytes 6152 | tf_op jit(solution)/shard_map/ppermute | solution.py:317
  43.3 1.2 %collective-permute-start.8 = (f32[1,512]{1,0:T(1,128)S(1)}, f32[1,512]{1,0:T(1,128)S(1)}, u32[]{:S(2)}, u32[]{:S(2)}) collective-permute-start(f32[1,512]{1,0:T(1,128)S(1)} %broadcast_select_fusion.6.entry), channel_id=1, source_target_pairs={{0,1},{1,0},{2,3},{3,2},{4,5},{5,4},{6,7},{7,6},{8,9},{9,8},{10,11... | collective-permute-start | bytes 6152 | tf_op jit(solution)/shard_map/ppermute | solution.py:329

commit v3 on v2

--- a/solution.py
+++ b/solution.py
@@ -25,11 +25,9 @@
 def product(left, right):
     lhi, llo = split(left)
     rhi, rlo = split(right)
-    return jnp.dot(
-        jnp.concatenate([lhi, llo, lhi], axis=1),
-        jnp.concatenate([rhi, rhi, rlo], axis=0),
-        preferred_element_type=F32,
-    )
+    both = jnp.dot(jnp.concatenate([lhi, llo], axis=0), rhi, preferred_element_type=F32)
+    rows = left.shape[0]
+    return both[:rows] + both[rows:] + jnp.dot(lhi, rlo, preferred_element_type=F32)
 
 
 def columns_of(row):
@@ -57,9 +55,9 @@
 
 def net_kernel(
     mean_h, spread_h, keep_h, obs_h, b_in_h, b_out_h, w_in_h, w_out_h,
-    pre, last, offsets,
+    steps, last, free,
     mean_ref, spread_ref, keep_ref, obs_ref, b_in, b_out, w_in, w_out,
-    turned, w_wide, base, wide, h0, h1, jac, pm, held_ref, sems, out_sems,
+    turned, w_wide, base, wide, h0, h1, jac, pm, known_ref, held_ref, sems, out_sems,
 ):
     n_steps, width = mean_ref.shape
     units = w_in.shape[1]
@@ -81,6 +79,7 @@
     for copy in copies[:6]:
         copy.wait()
 
+
     mean = mean_ref[...]
     centre_pts = mean.astype(BF16)
     centre_f = centre_pts.astype(F32)
@@ -96,19 +95,21 @@
     for b in range(0, width, LANES):
         turned[pl.ds(b, LANES), :] = jnp.transpose(stacked[:, b : b + LANES])
 
-    def widen(k):
+    def widen(k, kinds):
         for b in range(0, width, LANES):
-            for a in range(4):
+            for a in kinds:
                 at = a * n_steps + k
                 block = jnp.broadcast_to(turned[pl.ds(b, LANES), at : at + 1], (LANES, LANES))
                 if a == 3:
                     block = jnp.where(eye, block, 0.0)
                 wide[a, k, pl.ds(b, LANES), :] = block
 
-    widen(0)
+    widen(0, (0, 1))
 
     def gelu(k, j0, dst):
         for c in range(0, units, 256):
+            if k == 0 and j0 == 0 and c == 3 * quarter:
+                copies[10].wait()
             if k == 0 and j0 == 0 and c % quarter == 0:
                 copies[6 + c // quarter].wait()
                 part = pl.ds(c, quarter)
@@ -151,59 +152,72 @@
             held_ref[k] = held
         else:
             last[pl.ds(0, width), :] = held
-        if k < n_steps - 1:
-            sends.append(pltpu.make_async_copy(held_ref.at[k], pre.at[k], out_sems.at[k]))
-            sends[-1].start()
-
+
+    points = 2.0 * width
     slots = (h0, h1)
     tiles = 2 * n_steps
     for tile in range(tiles + 1):
-        if tile < tiles:
-            gelu(tile // 2, (tile % 2) * half, slots[tile % 2])
-        if tile % 2 == 0 and tile + 2 < tiles:
-            widen(tile // 2 + 1)
-        if tile == 0:
-            copies[10].wait()
+        if tile == tiles - 1:
+            for k in range(n_steps - 1):
+                sends.append(pltpu.make_async_copy(jac.at[k], steps.at[k], out_sems.at[k]))
+                sends[-1].start()
         if tile > 0:
             k, side = (tile - 1) // 2, (tile - 1) % 2
             total = outer(k, side * half, slots[side])
             pm[pl.ds(k, 1), :] = total if side == 0 else pm[pl.ds(k, 1), :] + total
-        if tile == 3:
-            sends.append(pltpu.make_async_copy(jac.at[0], pre.at[0], out_sems.at[0]))
-            sends[-1].start()
         if tile >= 5 and tile % 2 == 1:
             compose((tile - 3) // 2)
-
-    points = 2.0 * width
-    y = base[...]
-    z = y * (y * y * (8.0 * C1) + 2.0 * C0)
-    hidden = (y * jnp.tanh(z) + y).astype(BF16)
-    centre = jnp.dot(hidden, w_out[...], preferred_element_type=F32) + b_out[...] + centre_f
-    sums = pm[pl.ds(0, n_steps), :] + points * b_out[...] + ((points - 2.0) * centre_f + (up + lo))
-    point_mean = centre / (width + 1.0) + sums / (2.0 * (width + 1.0))
-    keep = keep_ref[...]
-    free = keep * point_mean + (1.0 - keep) * obs_ref[...]
-    consts = []
-    for k in range(n_steps):
-        moved = row_times(columns_of(mean[k : k + 1]), lambda r, c: jac[k, r, c])
-        consts.append(free[k : k + 1] - moved)
-
+        if tile < tiles:
+            gelu(tile // 2, (tile % 2) * half, slots[tile % 2])
+        if tile == 0:
+            widen(0, (2, 3))
+        if tile == 2:
+            y = base[...]
+            z = y * (y * y * (8.0 * C1) + 2.0 * C0)
+            hidden = (y * jnp.tanh(z) + y).astype(BF16)
+            centre = jnp.dot(hidden, w_out[...], preferred_element_type=F32) + b_out[...] + centre_f
+            keep = keep_ref[...]
+            known = keep * (
+                centre / (width + 1.0)
+                + (points * b_out[...] + ((points - 2.0) * centre_f + (up + lo))) / (2.0 * (width + 1.0))
+            ) + (1.0 - keep) * obs_ref[...]
+            known_ref[pl.ds(0, n_steps), :] = known
+        if tile % 2 == 0 and tile + 2 < tiles:
+            widen(tile // 2 + 1, (0, 1, 2, 3))
     for k in range((tiles - 3) // 2 + 1, n_steps):
         compose(k)
-    const = consts[0]
-    offsets[pl.ds(0, 1), :] = const
-    for k in range(1, n_steps):
-        const = row_times(columns_of(const), lambda r, c: jac[k, r, c]) + consts[k]
-        offsets[pl.ds(k, 1), :] = const
+    const = jnp.zeros((1, width), F32)
+    for k in range(n_steps):
+        row = pl.ds(k, 1)
+        own = known_ref[row, :] + keep_ref[row, :] * (pm[row, :] / (2.0 * (width + 1.0)))
+        free[row, :] = own
+        const = row_times(columns_of(const - mean_ref[row, :]), lambda r, c: jac[k, r, c]) + own
     last[pl.ds(width, 8), :] = jnp.concatenate([const, jnp.zeros((7, width), F32)], axis=0)
     for send in sends:
         send.wait()
 
 
-def fetch_kernel(source, target, sem):
-    copy = pltpu.make_async_copy(source, target, sem)
-    copy.start()
-    copy.wait()
+def fetch_kernel(count, *refs):
+    sources, targets, sems = refs[:count], refs[-1 - count : -1], refs[-1]
+    copies = [
+        pltpu.make_async_copy(source, target, sems.at[i])
+        for i, (source, target) in enumerate(zip(sources, targets))
+    ]
+    for copy in copies:
+        copy.start()
+    for copy in copies:
+        copy.wait()
+
+
+def fetch(arrays, after=()):
+    return pl.pallas_call(
+        functools.partial(fetch_kernel, len(arrays)),
+        out_shape=tuple(jax.ShapeDtypeStruct(x.shape, x.dtype) for x in arrays),
+        in_specs=[HBM] * len(arrays) + [VMEM] * len(after),
+        out_specs=(VMEM,) * len(arrays),
+        scratch_shapes=[pltpu.SemaphoreType.DMA((len(arrays),))],
+        compiler_params=params(16),
+    )(*arrays, *after)
 
 
 def first_kernel(early, late, entry, leaving):
@@ -220,28 +234,30 @@
     chip[pl.ds(width, 8), :] = jnp.broadcast_to(const, (8, width))
 
 
-def hop_kernel(chip, entry, leaving):
+def hop_kernel(chip_at, chip, held, moved, *refs):
+    entry, leaving = refs[-2:]
     width = chip.shape[1]
-    leaving[...] = row_times(columns_of(entry[...]), lambda r, c: chip[r, c]) + chip[pl.ds(width, 1), :]
-
-
-def final_kernel(early, pre_h, last, offsets_h, entry, other, late_mask, out, pre, offsets, sems):
-    n_steps, width = offsets.shape
-    gets = [pltpu.make_async_copy(pre_h.at[k], pre.at[k], sems.at[k]) for k in range(n_steps - 1)]
-    gets.append(pltpu.make_async_copy(offsets_h, offsets, sems.at[n_steps - 1]))
-    for get in gets:
-        get.start()
+    arrived = lax.axis_index("tm") == 2 * chip_at + 1
+    row = jnp.where(arrived, moved[...], held[...])
+    entry[...] = row
+    leaving[...] = row_times(columns_of(row), lambda r, c: chip[r, c]) + chip[pl.ds(width, 1), :]
+
+
+def arrive_kernel(chip_at, held, moved, entry):
+    entry[...] = jnp.where(lax.axis_index("tm") == 2 * chip_at + 1, moved[...], held[...])
+
+
+def final_kernel(early, steps, last, free, mean, entry, other, out):
+    n_steps, width = free.shape
     mid = row_times(columns_of(entry[...]), lambda r, c: early[r, c]) + early[pl.ds(width, 1), :]
-    begin = jnp.where(late_mask[...] > 0.0, mid, other[...])
-    cols = columns_of(begin)
-    gets[n_steps - 1].wait()
-    for k in range(n_steps):
-        if k < n_steps - 1:
-            gets[k].wait()
-            moved = row_times(cols, lambda r, c: pre[k, r, c])
-        else:
-            moved = row_times(cols, lambda r, c: last[r, c])
-        out[pl.ds(k, 1), :] = moved + offsets[pl.ds(k, 1), :]
+    state = jnp.where(lax.axis_index("tm") % 2 == 1, mid, other[...])
+    out[pl.ds(n_steps - 1, 1), :] = (
+        row_times(columns_of(state), lambda r, c: last[r, c]) + last[pl.ds(width, 1), :]
+    )
+    for k in range(n_steps - 1):
+        row = pl.ds(k, 1)
+        state = row_times(columns_of(state - mean[row, :]), lambda r, c: steps[k, r, c]) + free[row, :]
+        out[row, :] = state
 
 
 def params(mib):
@@ -252,11 +268,10 @@
     n_steps, width = lin_mean.shape
     units = w_in.shape[1]
     size = lax.axis_size("tm")
-    position = lax.axis_index("tm")
     shape = jax.ShapeDtypeStruct
 
     small = pltpu.VMEM((n_steps, width), F32)
-    pre, last, offsets = pl.pallas_call(
+    steps, last, free = pl.pallas_call(
         net_kernel,
         out_shape=(
             shape((n_steps - 1, width, width), F32),
@@ -279,6 +294,7 @@
             pltpu.VMEM((width, units), BF16),
             pltpu.VMEM((n_steps, width, width), F32),
             pltpu.VMEM((8, width), F32),
+            pltpu.VMEM((8, width), F32),
             pltpu.VMEM((n_steps - 1, width, width), F32),
             pltpu.SemaphoreType.DMA((11,)),
             pltpu.SemaphoreType.DMA((n_steps,)),
@@ -289,14 +305,7 @@
     swap = [(i, i ^ 1) for i in range(size)]
     row = start.reshape(1, width)
     early = lax.ppermute(last, "tm", swap)
-    late = pl.pallas_call(
-        fetch_kernel,
-        out_shape=shape((width + 8, width), F32),
-        in_specs=[HBM],
-        out_specs=VMEM,
-        scratch_shapes=[pltpu.SemaphoreType.DMA],
-        compiler_params=params(16),
-    )(last)
+    (late,) = fetch((last,))
     leaving = pl.pallas_call(
         first_kernel,
         out_shape=shape((1, width), F32),
@@ -311,35 +320,40 @@
         out_specs=VMEM,
         compiler_params=params(16),
     )(early, late)
+    row_shape = shape((1, width), F32)
     entry = row
     for chip_at in range(1, size // 2):
         if chip_at % 2 == 1 and size % 4 == 0:
             moved = lax.ppermute(leaving, "tm", [(i, i ^ 2) for i in range(size)])
         else:
             moved = lax.ppermute(leaving, "tm", [(2 * chip_at - 1, 2 * chip_at + 1)])
-        entry = jnp.where(position == 2 * chip_at + 1, moved, entry)
+        ready = (free,) if chip_at == 2 else ()
+        if chip_at == 1:
+            steps, free, lin_mean = fetch((steps, free, lin_mean), (moved,))
         if chip_at < size // 2 - 1:
-            leaving = pl.pallas_call(
-                hop_kernel,
-                out_shape=shape((1, width), F32),
+            entry, leaving = pl.pallas_call(
+                functools.partial(hop_kernel, chip_at),
+                out_shape=(row_shape, row_shape),
+                in_specs=[VMEM] * (3 + len(ready)),
+                out_specs=(VMEM, VMEM),
+                compiler_params=params(16),
+            )(chip, entry, moved, *ready)
+        else:
+            entry = pl.pallas_call(
+                functools.partial(arrive_kernel, chip_at),
+                out_shape=row_shape,
                 in_specs=[VMEM] * 2,
                 out_specs=VMEM,
                 compiler_params=params(16),
-            )(chip, entry)
+            )(entry, moved)
     other = lax.ppermute(entry, "tm", swap)
-    late_mask = jnp.broadcast_to((position % 2).astype(F32), (1, width))
     return pl.pallas_call(
         final_kernel,
         out_shape=shape((n_steps, width), F32),
-        in_specs=[VMEM, HBM, VMEM, HBM] + [VMEM] * 3,
+        in_specs=[VMEM] * 7,
         out_specs=VMEM,
-        scratch_shapes=[
-            pltpu.VMEM((n_steps - 1, width, width), F32),
-            pltpu.VMEM((n_steps, width), F32),
-            pltpu.SemaphoreType.DMA((n_steps,)),
-        ],
-        compiler_params=params(50),
-    )(early, pre, late, offsets, entry, other, late_mask)
+        compiler_params=params(16),
+    )(early, steps, late, free, lin_mean, entry, other)
 
 
 def solution(mesh):

time: 47.6 us -> 44.6 us (0.937)
  Pallas kernels: 24.3 us -> 21.8 us
    pallas_call x1, Pallas kernels: 2.75 us -> 1.26 us  [body(): pl.pallas_call(final_kernel, out_shape=shape((n_steps, width), F32), in_s...]
    pallas_call x1, Pallas kernels: 19.3 us -> 17.9 us  [body(): pl.pallas_call(net_kernel, out_shape=(shape((n_steps - 1, width, width),...]
    pallas_call x7 -> x9, Pallas kernels: 0.99 us -> 1.3 us  [the longest x6 0.93 us: body(): pl.pallas_call(functools.partial(hop_kernel, chip_at), out_shape=(row_sha...]
    unnamed x6 -> x10, local copies, waits for them, and re-layouts: 1.24 us -> 1.25 us
  transfers between devices with their start and end apart: 9 -> 9, of which waited for: 7 -> 7; matrix products, arithmetic and copies ran while one was open for 0% -> 0% of each run, Pallas kernels for 2% -> 3%
where the time goes in v3:
time: 44.6 us; the launch traced here: 44.4 us
  Pallas kernels  21.8 us (49%)
  waiting for transfers between devices  13.8 us (31%)
  starting transfers between devices  7.36 us (17%)
  local copies, waits for them, and re-layouts  1.25 us (3%)
    pallas_call x1, Pallas kernels, body(): pl.pallas_call(net_kernel, out_shape=(shape((n_steps - 1, width, width),...  17.9 us
    ppermute x3, waiting for transfers between devices, body(): moved = lax.ppermute(leaving, 'tm', [(2 * chip_at - 1, 2 * chip_at + 1)])  6.56 us
    ppermute x4, waiting for transfers between devices, body(): moved = lax.ppermute(leaving, 'tm', [(i, i ^ 2) for i in range(size)])  4.93 us
    ppermute x4, starting transfers between devices, body(): moved = lax.ppermute(leaving, 'tm', [(i, i ^ 2) for i in range(size)])  4.01 us
    ppermute x3, starting transfers between devices, body(): moved = lax.ppermute(leaving, 'tm', [(2 * chip_at - 1, 2 * chip_at + 1)])  2.62 us
    pallas_call x1, Pallas kernels, body(): pl.pallas_call(final_kernel, out_shape=shape((n_steps, width), F32), in_s...  1.26 us
    unnamed x10, local copies, waits for them, and re-layouts  1.25 us
    ppermute x1, waiting for transfers between devices, body(): early = lax.ppermute(last, 'tm', swap)  1.18 us
  transfers between devices with their start and end apart: 9, of which 7 were waited for; matrix products, arithmetic and copies ran while one was open for 0% of the time, Pallas kernels for 3%

profile of v3, /device:TPU:27, one launch (start us, length us, event | category | flops | bytes accessed | tf_op | source)
XLA Modules:
  0.0 44.4 jit_solution(17495359338267869789)
XLA Ops:
  0.0 17.9 %shard_map.91 = (f32[3,512,512]{2,1,0:T(8,128)}, f32[520,512]{1,0:T(8,128)}, f32[4,512]{1,0:T(4,128)}) custom-call(f32[4,512]{1,0:T(4,128)} %refs_2_.1, f32[4,512]{1,0:T(4,128)} %spread_h.1, f32[4,512]{1,0:T(4,128)} %keep_h.1, f32[4,512]{1,0:T(4,128)} %obs_h.1, f32[1,2048]{1,0:T(1,128)} %bitcast.5, f32[1,512]{1,0:T(1,128)} %bitcast.6, ...), custom_call_target="tpu_custom_call" | custom-call | tf_op jit(solution)/shard_map/pallas_call | solution.py:274
  17.9 0.7 %collective-permute-start = (f32[520,512]{1,0:T(8,128)}, f32[520,512]{1,0:T(8,128)S(1)}, u32[]{:S(2)}, u32[]{:S(2)}) collective-permute-start(f32[520,512]{1,0:T(8,128)} %get-tuple-element.23.refs_0_), channel_id=1, source_target_pairs={{0,1},{1,0},{2,3},{3,2},{4,5},{5,4},{6,7},{7,6},{8,9},{9,8},{10,11... | collective-permute-start | bytes 3194888 | tf_op jit(solution)/shard_map/ppermute | solution.py:307
  18.7 1.2 %copy-done.1 = f32[520,512]{1,0:T(8,128)S(1)} copy-done((f32[520,512]{1,0:T(8,128)S(1)}, f32[520,512]{1,0:T(8,128)}, u32[]{:S(2)}) %copy-start.1) | copy-done | bytes 1064984
  19.9 0.1 shard_map.92.late.last
  20.0 1.2 %collective-permute-done.early = f32[520,512]{1,0:T(8,128)S(1)} collective-permute-done((f32[520,512]{1,0:T(8,128)}, f32[520,512]{1,0:T(8,128)S(1)}, u32[]{:S(2)}, u32[]{:S(2)}) %collective-permute-start) | collective-permute-done | bytes 1064992 | tf_op jit(solution)/shard_map/ppermute | solution.py:307
  21.2 0.3 shard_map.93
  21.5 0.0 copy-start.2
  21.5 0.0 copy-start.3
  21.5 1.3 %collective-permute-start.1 = (f32[1,512]{1,0:T(1,128)S(1)}, f32[1,512]{1,0:T(1,128)S(1)}, u32[]{:S(2)}, u32[]{:S(2)}) collective-permute-start(f32[1,512]{1,0:T(1,128)S(1)} %shard_map.93), channel_id=1, source_target_pairs={{0,2},{1,3},{2,0},{3,1},{4,6},{5,7},{6,4},{7,5},{8,10},{9,11},{10,... | collective-permute-start | bytes 6152 | tf_op jit(solution)/shard_map/ppermute | solution.py:327
  22.8 1.0 %shard_map.95.chip = f32[520,512]{1,0:T(8,128)S(1)} custom-call(f32[520,512]{1,0:T(8,128)S(1)} %collective-permute-done.early, f32[520,512]{1,0:T(8,128)S(1)} %shard_map.92.late.last), custom_call_target="tpu_custom_call" | custom-call | tf_op jit(solution)/shard_map/pallas_call | solution.py:316
  23.9 0.1 collective-permute-done.1.refs_3_.moved
  24.0 0.2 shard_map.96
  24.2 0.7 %collective-permute-start.2 = (f32[1,512]{1,0:T(1,128)S(1)}, f32[1,512]{1,0:T(1,128)S(1)}, u32[]{:S(2)}, u32[]{:S(2)}) collective-permute-start(f32[1,512]{1,0:T(1,128)S(1)} %get-tuple-element.30), channel_id=1, source_target_pairs={{3,5},{19,21}} | collective-permute-start | bytes 6152 | tf_op jit(solution)/shard_map/ppermute | solution.py:329
  24.9 0.3 shard_map.94
  25.1 0.0 collective-permute-done.2.moved
  25.2 0.2 shard_map.97
  25.3 1.3 %collective-permute-start.3 = (f32[1,512]{1,0:T(1,128)S(1)}, f32[1,512]{1,0:T(1,128)S(1)}, u32[]{:S(2)}, u32[]{:S(2)}) collective-permute-start(f32[1,512]{1,0:T(1,128)S(1)} %get-tuple-element.32), channel_id=1, source_target_pairs={{0,2},{1,3},{2,0},{3,1},{4,6},{5,7},{6,4},{7,5},{8,10},{9,11},{10,... | collective-permute-start | bytes 6152 | tf_op jit(solution)/shard_map/ppermute | solution.py:327
  26.6 1.2 %collective-permute-done.3.moved = f32[1,512]{1,0:T(1,128)S(1)} collective-permute-done((f32[1,512]{1,0:T(1,128)S(1)}, f32[1,512]{1,0:T(1,128)S(1)}, u32[]{:S(2)}, u32[]{:S(2)}) %collective-permute-start.3) | collective-permute-done | bytes 2080 | tf_op jit(solution)/shard_map/ppermute | solution.py:327
  27.8 0.2 shard_map.98
  28.0 0.7 %collective-permute-start.4 = (f32[1,512]{1,0:T(1,128)S(1)}, f32[1,512]{1,0:T(1,128)S(1)}, u32[]{:S(2)}, u32[]{:S(2)}) collective-permute-start(f32[1,512]{1,0:T(1,128)S(1)} %get-tuple-element.34), channel_id=1, source_target_pairs={{7,9},{23,25}} | collective-permute-start | bytes 6152 | tf_op jit(solution)/shard_map/ppermute | solution.py:329
  28.6 0.0 collective-permute-done.4.moved
  28.7 0.2 shard_map.99
  28.8 1.3 %collective-permute-start.5 = (f32[1,512]{1,0:T(1,128)S(1)}, f32[1,512]{1,0:T(1,128)S(1)}, u32[]{:S(2)}, u32[]{:S(2)}) collective-permute-start(f32[1,512]{1,0:T(1,128)S(1)} %get-tuple-element.36), channel_id=1, source_target_pairs={{0,2},{1,3},{2,0},{3,1},{4,6},{5,7},{6,4},{7,5},{8,10},{9,11},{10,... | collective-permute-start | bytes 6152 | tf_op jit(solution)/shard_map/ppermute | solution.py:327
  30.1 1.2 %collective-permute-done.5.moved = f32[1,512]{1,0:T(1,128)S(1)} collective-permute-done((f32[1,512]{1,0:T(1,128)S(1)}, f32[1,512]{1,0:T(1,128)S(1)}, u32[]{:S(2)}, u32[]{:S(2)}) %collective-permute-start.5) | collective-permute-done | bytes 2080 | tf_op jit(solution)/shard_map/ppermute | solution.py:327
  31.3 0.2 shard_map.100
  31.5 1.3 %collective-permute-start.6 = (f32[1,512]{1,0:T(1,128)S(1)}, f32[1,512]{1,0:T(1,128)S(1)}, u32[]{:S(2)}, u32[]{:S(2)}) collective-permute-start(f32[1,512]{1,0:T(1,128)S(1)} %get-tuple-element.38), channel_id=1, source_target_pairs={{11,13},{27,29}} | collective-permute-start | bytes 6152 | tf_op jit(solution)/shard_map/ppermute | solution.py:329
  32.8 6.6 %collective-permute-done.6.moved = f32[1,512]{1,0:T(1,128)S(1)} collective-permute-done((f32[1,512]{1,0:T(1,128)S(1)}, f32[1,512]{1,0:T(1,128)S(1)}, u32[]{:S(2)}, u32[]{:S(2)}) %collective-permute-start.6) | collective-permute-done | bytes 2080 | tf_op jit(solution)/shard_map/ppermute | solution.py:329
  39.3 0.2 shard_map.101
  39.5 0.1 collective-permute-start.7
  39.6 2.4 %collective-permute-done.7.moved = f32[1,512]{1,0:T(1,128)S(1)} collective-permute-done((f32[1,512]{1,0:T(1,128)S(1)}, f32[1,512]{1,0:T(1,128)S(1)}, u32[]{:S(2)}, u32[]{:S(2)}) %collective-permute-start.7) | collective-permute-done | bytes 2080 | tf_op jit(solution)/shard_map/ppermute | solution.py:327
  42.0 1.2 %collective-permute-done.8.other = f32[1,512]{1,0:T(1,128)S(1)} collective-permute-done((f32[1,512]{1,0:T(1,128)S(1)}, f32[1,512]{1,0:T(1,128)S(1)}, u32[]{:S(2)}, u32[]{:S(2)}) %collective-permute-start.8) | collective-permute-done | bytes 2080 | tf_op jit(solution)/shard_map/ppermute | solution.py:349
  43.1 1.3 %shard_map.103 = f32[4,512]{1,0:T(4,128)} custom-call(f32[520,512]{1,0:T(8,128)S(1)} %collective-permute-done.early, f32[3,512,512]{2,1,0:T(8,128)S(1)} %get-tuple-element.26.steps, f32[520,512]{1,0:T(8,128)S(1)} %shard_map.92.late.last, f32[4,512]{1,0:T(4,128)S(1)} %get-tuple-element.27.refs_0_.free, f32[4,512]{1,0:T(4,128)S(1)} %get-tuple-element.28.mean, ...), custom_call_target="tpu_custom_call" | custom-call | tf_op jit(solution)/shard_map/pallas_call | solution.py:350
  (9 shorter events, 0.0 us)
Async XLA Ops:
  0.0 21.2 %copy-start.4 = (f32[512]{0:T(512)S(1)}, f32[512]{0:T(512)}, u32[]{:S(2)}) copy-start(f32[512]{0:T(512)} %param.13) | copy-start | bytes 6148
  17.9 3.3 %collective-permute-start = (f32[520,512]{1,0:T(8,128)}, f32[520,512]{1,0:T(8,128)S(1)}, u32[]{:S(2)}, u32[]{:S(2)}) collective-permute-start(f32[520,512]{1,0:T(8,128)} %get-tuple-element.23.refs_0_), channel_id=1, source_target_pairs={{0,1},{1,0},{2,3},{3,2},{4,5},{5,4},{6,7},{7,6},{8,9},{9,8},{10,11... | collective-permute-start | bytes 3194888 | tf_op jit(solution)/shard_map/ppermute | solution.py:307
  18.7 1.2 %copy-start.1 = (f32[520,512]{1,0:T(8,128)S(1)}, f32[520,512]{1,0:T(8,128)}, u32[]{:S(2)}) copy-start(f32[520,512]{1,0:T(8,128)} %get-tuple-element.23.refs_0_) | copy-start | bytes 3194884
  21.5 3.4 %copy-start = (f32[3,512,512]{2,1,0:T(8,128)S(1)}, f32[3,512,512]{2,1,0:T(8,128)}, u32[]{:S(2)}) copy-start(f32[3,512,512]{2,1,0:T(8,128)} %get-tuple-element.24.refs_0_) | copy-start | bytes 9437188
  21.5 3.4 %copy-start.2 = (f32[4,512]{1,0:T(4,128)S(1)}, f32[4,512]{1,0:T(4,128)}, u32[]{:S(2)}) copy-start(f32[4,512]{1,0:T(4,128)} %refs_2_.1) | copy-start | bytes 24580
  21.5 3.4 %copy-start.3 = (f32[4,512]{1,0:T(4,128)S(1)}, f32[4,512]{1,0:T(4,128)}, u32[]{:S(2)}) copy-start(f32[4,512]{1,0:T(4,128)} %get-tuple-element.25.refs_1_) | copy-start | bytes 24580
  21.5 2.5 %collective-permute-start.1 = (f32[1,512]{1,0:T(1,128)S(1)}, f32[1,512]{1,0:T(1,128)S(1)}, u32[]{:S(2)}, u32[]{:S(2)}) collective-permute-start(f32[1,512]{1,0:T(1,128)S(1)} %shard_map.93), channel_id=1, source_target_pairs={{0,2},{1,3},{2,0},{3,1},{4,6},{5,7},{6,4},{7,5},{8,10},{9,11},{10,... | collective-permute-start | bytes 6152 | tf_op jit(solution)/shard_map/ppermute | solution.py:327
  24.2 1.0 %collective-permute-start.2 = (f32[1,512]{1,0:T(1,128)S(1)}, f32[1,512]{1,0:T(1,128)S(1)}, u32[]{:S(2)}, u32[]{:S(2)}) collective-permute-start(f32[1,512]{1,0:T(1,128)S(1)} %get-tuple-element.30), channel_id=1, source_target_pairs={{3,5},{19,21}} | collective-permute-start | bytes 6152 | tf_op jit(solution)/shard_map/ppermute | solution.py:329
  25.3 2.5 %collective-permute-start.3 = (f32[1,512]{1,0:T(1,128)S(1)}, f32[1,512]{1,0:T(1,128)S(1)}, u32[]{:S(2)}, u32[]{:S(2)}) collective-permute-start(f32[1,512]{1,0:T(1,128)S(1)} %get-tuple-element.32), channel_id=1, source_target_pairs={{0,2},{1,3},{2,0},{3,1},{4,6},{5,7},{6,4},{7,5},{8,10},{9,11},{10,... | collective-permute-start | bytes 6152 | tf_op jit(solution)/shard_map/ppermute | solution.py:327
  28.0 0.7 %collective-permute-start.4 = (f32[1,512]{1,0:T(1,128)S(1)}, f32[1,512]{1,0:T(1,128)S(1)}, u32[]{:S(2)}, u32[]{:S(2)}) collective-permute-start(f32[1,512]{1,0:T(1,128)S(1)} %get-tuple-element.34), channel_id=1, source_target_pairs={{7,9},{23,25}} | collective-permute-start | bytes 6152 | tf_op jit(solution)/shard_map/ppermute | solution.py:329
  28.8 2.5 %collective-permute-start.5 = (f32[1,512]{1,0:T(1,128)S(1)}, f32[1,512]{1,0:T(1,128)S(1)}, u32[]{:S(2)}, u32[]{:S(2)}) collective-permute-start(f32[1,512]{1,0:T(1,128)S(1)} %get-tuple-element.36), channel_id=1, source_target_pairs={{0,2},{1,3},{2,0},{3,1},{4,6},{5,7},{6,4},{7,5},{8,10},{9,11},{10,... | collective-permute-start | bytes 6152 | tf_op jit(solution)/shard_map/ppermute | solution.py:327
  31.5 7.9 %collective-permute-start.6 = (f32[1,512]{1,0:T(1,128)S(1)}, f32[1,512]{1,0:T(1,128)S(1)}, u32[]{:S(2)}, u32[]{:S(2)}) collective-permute-start(f32[1,512]{1,0:T(1,128)S(1)} %get-tuple-element.38), channel_id=1, source_target_pairs={{11,13},{27,29}} | collective-permute-start | bytes 6152 | tf_op jit(solution)/shard_map/ppermute | solution.py:329
  39.5 2.5 %collective-permute-start.7 = (f32[1,512]{1,0:T(1,128)S(1)}, f32[1,512]{1,0:T(1,128)S(1)}, u32[]{:S(2)}, u32[]{:S(2)}) collective-permute-start(f32[1,512]{1,0:T(1,128)S(1)} %get-tuple-element.40), channel_id=1, source_target_pairs={{0,2},{1,3},{2,0},{3,1},{4,6},{5,7},{6,4},{7,5},{8,10},{9,11},{10,... | collective-permute-start | bytes 6152 | tf_op jit(solution)/shard_map/ppermute | solution.py:327
  42.0 1.2 %collective-permute-start.8 = (f32[1,512]{1,0:T(1,128)S(1)}, f32[1,512]{1,0:T(1,128)S(1)}, u32[]{:S(2)}, u32[]{:S(2)}) collective-permute-start(f32[1,512]{1,0:T(1,128)S(1)} %shard_map.102.entry), channel_id=1, source_target_pairs={{0,1},{1,0},{2,3},{3,2},{4,5},{5,4},{6,7},{7,6},{8,9},{9,8},{10,11... | collective-permute-start | bytes 6152 | tf_op jit(solution)/shard_map/ppermute | solution.py:349

commit v4 on v3

--- a/solution.py
+++ b/solution.py
@@ -54,17 +54,17 @@
 
 
 def net_kernel(
-    mean_h, spread_h, keep_h, obs_h, b_in_h, b_out_h, w_in_h, w_out_h,
-    steps, last, free,
-    mean_ref, spread_ref, keep_ref, obs_ref, b_in, b_out, w_in, w_out,
+    mean_h, spread_h, keep_h, obs_h, b_in_h, b_out_h, start_h, w_in_h, w_out_h,
+    steps, last, free, first,
+    mean_ref, spread_ref, keep_ref, obs_ref, b_in, b_out, start, w_in, w_out,
     turned, w_wide, base, wide, h0, h1, jac, pm, known_ref, held_ref, sems, out_sems,
 ):
     n_steps, width = mean_ref.shape
     units = w_in.shape[1]
     half = width // 2
     factor = math.sqrt(width + 1.0)
-    sources = (mean_h, spread_h, keep_h, obs_h, b_in_h, b_out_h)
-    targets = (mean_ref, spread_ref, keep_ref, obs_ref, b_in, b_out)
+    sources = (mean_h, spread_h, keep_h, obs_h, b_in_h, b_out_h, start_h)
+    targets = (mean_ref, spread_ref, keep_ref, obs_ref, b_in, b_out, start)
     copies = [
         pltpu.make_async_copy(source, target, sems.at[i])
         for i, (source, target) in enumerate(zip(sources, targets))
@@ -72,11 +72,11 @@
     quarter = units // 4
     for i in range(4):
         part = pl.ds(i * quarter, quarter)
-        copies.append(pltpu.make_async_copy(w_in_h.at[:, part], w_in.at[:, part], sems.at[6 + i]))
-    copies.append(pltpu.make_async_copy(w_out_h, w_out, sems.at[10]))
+        copies.append(pltpu.make_async_copy(w_in_h.at[:, part], w_in.at[:, part], sems.at[7 + i]))
+    copies.append(pltpu.make_async_copy(w_out_h, w_out, sems.at[11]))
     for copy in copies:
         copy.start()
-    for copy in copies[:6]:
+    for copy in copies[:7]:
         copy.wait()
 
 
@@ -109,9 +109,9 @@
     def gelu(k, j0, dst):
         for c in range(0, units, 256):
             if k == 0 and j0 == 0 and c == 3 * quarter:
-                copies[10].wait()
+                copies[11].wait()
             if k == 0 and j0 == 0 and c % quarter == 0:
-                copies[6 + c // quarter].wait()
+                copies[7 + c // quarter].wait()
                 part = pl.ds(c, quarter)
                 base[:, part] = (
                     jnp.dot(centre_pts, w_in[:, part], preferred_element_type=F32) + b_in[:, part]
@@ -193,6 +193,7 @@
         free[row, :] = own
         const = row_times(columns_of(const - mean_ref[row, :]), lambda r, c: jac[k, r, c]) + own
     last[pl.ds(width, 8), :] = jnp.concatenate([const, jnp.zeros((7, width), F32)], axis=0)
+    first[...] = row_times(columns_of(start[...]), lambda r, c: last[r, c]) + const
     for send in sends:
         send.wait()
 
@@ -220,9 +221,16 @@
     )(*arrays, *after)
 
 
-def first_kernel(early, late, entry, leaving):
+def first_kernel(late, entry, leaving):
     width = late.shape[1]
-    mid = row_times(columns_of(entry[...]), lambda r, c: early[r, c]) + early[pl.ds(width, 1), :]
+    leaving[...] = row_times(columns_of(entry[...]), lambda r, c: late[r, c]) + late[pl.ds(width, 1), :]
+
+
+def second_kernel(early, late, held, moved, entry, leaving):
+    width = late.shape[1]
+    row = jnp.where(lax.axis_index("tm") == 3, moved[...], held[...])
+    entry[...] = row
+    mid = row_times(columns_of(row), lambda r, c: early[r, c]) + early[pl.ds(width, 1), :]
     leaving[...] = row_times(columns_of(mid), lambda r, c: late[r, c]) + late[pl.ds(width, 1), :]
 
 
@@ -247,17 +255,25 @@
     entry[...] = jnp.where(lax.axis_index("tm") == 2 * chip_at + 1, moved[...], held[...])
 
 
-def final_kernel(early, steps, last, free, mean, entry, other, out):
+def final_kernel(chosen, early, steps, last, free, mean, entry, other, *refs):
+    out, rows, sem = refs[-3:]
     n_steps, width = free.shape
-    mid = row_times(columns_of(entry[...]), lambda r, c: early[r, c]) + early[pl.ds(width, 1), :]
-    state = jnp.where(lax.axis_index("tm") % 2 == 1, mid, other[...])
-    out[pl.ds(n_steps - 1, 1), :] = (
-        row_times(columns_of(state), lambda r, c: last[r, c]) + last[pl.ds(width, 1), :]
-    )
-    for k in range(n_steps - 1):
-        row = pl.ds(k, 1)
-        state = row_times(columns_of(state - mean[row, :]), lambda r, c: steps[k, r, c]) + free[row, :]
-        out[row, :] = state
+    place = lax.axis_index("tm")
+
+    @pl.when(chosen(place // 2))
+    def _():
+        mid = row_times(columns_of(entry[...]), lambda r, c: early[r, c]) + early[pl.ds(width, 1), :]
+        state = jnp.where(place % 2 == 1, mid, other[...])
+        rows[pl.ds(n_steps - 1, 1), :] = (
+            row_times(columns_of(state), lambda r, c: last[r, c]) + last[pl.ds(width, 1), :]
+        )
+        for k in range(n_steps - 1):
+            row = pl.ds(k, 1)
+            state = row_times(columns_of(state - mean[row, :]), lambda r, c: steps[k, r, c]) + free[row, :]
+            rows[row, :] = state
+        copy = pltpu.make_async_copy(rows, out, sem)
+        copy.start()
+        copy.wait()
 
 
 def params(mib):
@@ -271,18 +287,21 @@
     shape = jax.ShapeDtypeStruct
 
     small = pltpu.VMEM((n_steps, width), F32)
-    steps, last, free = pl.pallas_call(
+    row = start.reshape(1, width)
+    steps, last, free, first = pl.pallas_call(
         net_kernel,
         out_shape=(
             shape((n_steps - 1, width, width), F32),
             shape((width + 8, width), F32),
             shape((n_steps, width), F32),
+            shape((1, width), F32),
         ),
-        in_specs=[HBM] * 8,
-        out_specs=(HBM, VMEM, VMEM),
+        in_specs=[HBM] * 9,
+        out_specs=(HBM, VMEM, VMEM, VMEM),
         scratch_shapes=[
             small, small, small, small,
             pltpu.VMEM((1, units), F32),
+            pltpu.VMEM((1, width), F32),
             pltpu.VMEM((1, width), F32),
             pltpu.VMEM((width, units), BF16),
             pltpu.VMEM((units, width), BF16),
@@ -296,23 +315,24 @@
             pltpu.VMEM((8, width), F32),
             pltpu.VMEM((8, width), F32),
             pltpu.VMEM((n_steps - 1, width, width), F32),
-            pltpu.SemaphoreType.DMA((11,)),
+            pltpu.SemaphoreType.DMA((12,)),
             pltpu.SemaphoreType.DMA((n_steps,)),
         ],
         compiler_params=params(60),
-    )(lin_mean, spread, keep, observed, b_in.reshape(1, units), b_out.reshape(1, width), w_in, w_out)
+    )(lin_mean, spread, keep, observed, b_in.reshape(1, units), b_out.reshape(1, width), row, w_in, w_out)
 
     swap = [(i, i ^ 1) for i in range(size)]
-    row = start.reshape(1, width)
-    early = lax.ppermute(last, "tm", swap)
+    halfway = lax.ppermute(first, "tm", swap)
     (late,) = fetch((last,))
+    (sent,) = fetch((late,), (halfway,))
+    early = lax.ppermute(sent, "tm", swap)
     leaving = pl.pallas_call(
         first_kernel,
         out_shape=shape((1, width), F32),
-        in_specs=[VMEM] * 3,
+        in_specs=[VMEM] * 2,
         out_specs=VMEM,
         compiler_params=params(16),
-    )(early, late, row)
+    )(late, halfway)
     chip = pl.pallas_call(
         pair_kernel,
         out_shape=shape((width + 8, width), F32),
@@ -321,8 +341,22 @@
         compiler_params=params(16),
     )(early, late)
     row_shape = shape((1, width), F32)
+    chips = size // 2
+    kept = ()
+
+    def finish(chosen, entry, other, kept):
+        return pl.pallas_call(
+            functools.partial(final_kernel, chosen),
+            out_shape=shape((n_steps, width), F32),
+            in_specs=[VMEM] * 7 + [HBM] * len(kept),
+            out_specs=HBM,
+            input_output_aliases={7: 0} if kept else {},
+            scratch_shapes=[pltpu.VMEM((n_steps, width), F32), pltpu.SemaphoreType.DMA],
+            compiler_params=params(16),
+        )(early, steps, late, free, lin_mean, entry, other, *kept)
+
     entry = row
-    for chip_at in range(1, size // 2):
+    for chip_at in range(1, chips):
         if chip_at % 2 == 1 and size % 4 == 0:
             moved = lax.ppermute(leaving, "tm", [(i, i ^ 2) for i in range(size)])
         else:
@@ -330,7 +364,15 @@
         ready = (free,) if chip_at == 2 else ()
         if chip_at == 1:
             steps, free, lin_mean = fetch((steps, free, lin_mean), (moved,))
-        if chip_at < size // 2 - 1:
+        if chip_at == 1 and chips > 2:
+            entry, leaving = pl.pallas_call(
+                second_kernel,
+                out_shape=(row_shape, row_shape),
+                in_specs=[VMEM] * 4,
+                out_specs=(VMEM, VMEM),
+                compiler_params=params(16),
+            )(early, late, entry, moved)
+        elif chip_at < chips - 1:
             entry, leaving = pl.pallas_call(
                 functools.partial(hop_kernel, chip_at),
                 out_shape=(row_shape, row_shape),
@@ -339,6 +381,8 @@
                 compiler_params=params(16),
             )(chip, entry, moved, *ready)
         else:
+            other = lax.ppermute(entry, "tm", swap)
+            kept = (finish(lambda at: at < chips - 1, entry, other, ()),)
             entry = pl.pallas_call(
                 functools.partial(arrive_kernel, chip_at),
                 out_shape=row_shape,
@@ -347,13 +391,7 @@
                 compiler_params=params(16),
             )(entry, moved)
     other = lax.ppermute(entry, "tm", swap)
-    return pl.pallas_call(
-        final_kernel,
-        out_shape=shape((n_steps, width), F32),
-        in_specs=[VMEM] * 7,
-        out_specs=VMEM,
-        compiler_params=params(16),
-    )(early, steps, late, free, lin_mean, entry, other)
+    return finish(lambda at: at == chips - 1, entry, other, kept)
 
 
 def solution(mesh):

time: 44.6 us -> 42.9 us (0.962)
  waiting for transfers between devices: 13.8 us -> 11.5 us
    ppermute x1 -> x2, waiting for transfers between devices: 1.18 us -> 0.01 us  [the longest x1 0.01 us: body(): halfway = lax.ppermute(first, 'tm', swap)]
    ppermute x1 -> x2, waiting for transfers between devices: 1.15 us -> 0.01 us  [body(): other = lax.ppermute(entry, 'tm', swap)]
    ppermute x4, waiting for transfers between devices: 4.93 us -> 5.91 us  [body(): moved = lax.ppermute(leaving, 'tm', [(i, i ^ 2) for i in range(size)])]
    ppermute x3, waiting for transfers between devices: 6.56 us -> 5.62 us  [body(): moved = lax.ppermute(leaving, 'tm', [(2 * chip_at - 1, 2 * chip_at + 1)])]
    pallas_call x1 -> x3, Pallas kernels: 1.26 us -> 1.61 us  [the longest x2 1.31 us: finish(): pl.pallas_call(functools.partial(final_kernel, chosen), out_shape=shape((...]
    pallas_call x6 -> x5, Pallas kernels: 0.93 us -> 0.78 us  [body(): pl.pallas_call(functools.partial(hop_kernel, chip_at), out_shape=(row_sha...]
  transfers between devices with their start and end apart: 9 -> 11, of which waited for: 7 -> 5; matrix products, arithmetic and copies ran while one was open for 0% -> 0% of each run, Pallas kernels for 3% -> 7%
where the time goes in v4:
time: 42.9 us; the launch traced here: 42.7 us
  Pallas kernels  22 us (51%)
  waiting for transfers between devices  11.5 us (27%)
  starting transfers between devices  7.51 us (18%)
  local copies, waits for them, and re-layouts  1.25 us (3%)
    pallas_call x1, Pallas kernels, body(): pl.pallas_call(net_kernel, out_shape=(shape((n_steps - 1, width, width),...  17.9 us
    ppermute x4, waiting for transfers between devices, body(): moved = lax.ppermute(leaving, 'tm', [(i, i ^ 2) for i in range(size)])  5.91 us
    ppermute x3, waiting for transfers between devices, body(): moved = lax.ppermute(leaving, 'tm', [(2 * chip_at - 1, 2 * chip_at + 1)])  5.62 us
    ppermute x4, starting transfers between devices, body(): moved = lax.ppermute(leaving, 'tm', [(i, i ^ 2) for i in range(size)])  4.01 us
    ppermute x3, starting transfers between devices, body(): moved = lax.ppermute(leaving, 'tm', [(2 * chip_at - 1, 2 * chip_at + 1)])  2.62 us
    pallas_call x2, Pallas kernels, finish(): pl.pallas_call(functools.partial(final_kernel, chosen), out_shape=shape((...  1.31 us
    unnamed x10, local copies, waits for them, and re-layouts  1.25 us
    pallas_call x1, Pallas kernels, body(): pl.pallas_call(pair_kernel, out_shape=shape((width + 8, width), F32), in_...  1.05 us
  transfers between devices with their start and end apart: 11, of which 5 were waited for; matrix products, arithmetic and copies ran while one was open for 0% of the time, Pallas kernels for 7%

profile of v4, /device:TPU:27, one launch (start us, length us, event | category | flops | bytes accessed | tf_op | source)
XLA Modules:
  0.0 42.7 jit_solution(14384579107070249542)
XLA Ops:
  0.0 17.9 %shard_map.91 = (f32[3,512,512]{2,1,0:T(8,128)}, f32[520,512]{1,0:T(8,128)}, f32[4,512]{1,0:T(4,128)}, f32[1,512]{1,0:T(1,128)}) custom-call(f32[4,512]{1,0:T(4,128)} %refs_2_.1, f32[4,512]{1,0:T(4,128)} %spread_h.1, f32[4,512]{1,0:T(4,128)} %keep_h.1, f32[4,512]{1,0:T(4,128)} %obs_h.1, f32[1,2048]{1,0:T(1,128)} %bitcast.5, f32[1,512]{1,0:T(1,128)} %bitcast.6, ...), custom_call_target="tpu_custom_call" | custom-call | tf_op jit(solution)/shard_map/pallas_call | solution.py:291
  17.9 0.7 %collective-permute-start = (f32[1,512]{1,0:T(1,128)}, f32[1,512]{1,0:T(1,128)S(1)}, u32[]{:S(2)}, u32[]{:S(2)}) collective-permute-start(f32[1,512]{1,0:T(1,128)} %get-tuple-element.25), channel_id=1, source_target_pairs={{0,1},{1,0},{2,3},{3,2},{4,5},{5,4},{6,7},{7,6},{8,9},{9,8},{10,11... | collective-permute-start | bytes 6152 | tf_op jit(solution)/shard_map/ppermute | solution.py:325
  18.7 1.2 %copy-done.1 = f32[520,512]{1,0:T(8,128)S(1)} copy-done((f32[520,512]{1,0:T(8,128)S(1)}, f32[520,512]{1,0:T(8,128)}, u32[]{:S(2)}) %copy-start.1) | copy-done | bytes 1064984
  19.9 0.1 shard_map.92.refs_0_.late.last
  20.0 0.1 shard_map.93
  20.1 0.0 copy-start.3
  20.1 0.1 collective-permute-start.1
  20.2 0.1 shard_map.94
  20.4 0.0 copy-start.2
  20.4 0.0 copy-start.4
  20.4 1.3 %collective-permute-start.2 = (f32[1,512]{1,0:T(1,128)S(1)}, f32[1,512]{1,0:T(1,128)S(1)}, u32[]{:S(2)}, u32[]{:S(2)}) collective-permute-start(f32[1,512]{1,0:T(1,128)S(1)} %shard_map.94), channel_id=1, source_target_pairs={{0,2},{1,3},{2,0},{3,1},{4,6},{5,7},{6,4},{7,5},{8,10},{9,11},{10,... | collective-permute-start | bytes 6152 | tf_op jit(solution)/shard_map/ppermute | solution.py:361
  21.7 1.2 %collective-permute-done.2.refs_3_.moved = f32[1,512]{1,0:T(1,128)S(1)} collective-permute-done((f32[1,512]{1,0:T(1,128)S(1)}, f32[1,512]{1,0:T(1,128)S(1)}, u32[]{:S(2)}, u32[]{:S(2)}) %collective-permute-start.2) | collective-permute-done | bytes 2080 | tf_op jit(solution)/shard_map/ppermute | solution.py:361
  22.9 0.3 shard_map.97
  23.2 0.7 %collective-permute-start.3 = (f32[1,512]{1,0:T(1,128)S(1)}, f32[1,512]{1,0:T(1,128)S(1)}, u32[]{:S(2)}, u32[]{:S(2)}) collective-permute-start(f32[1,512]{1,0:T(1,128)S(1)} %get-tuple-element.32), channel_id=1, source_target_pairs={{3,5},{19,21}} | collective-permute-start | bytes 6152 | tf_op jit(solution)/shard_map/ppermute | solution.py:363
  23.9 0.3 shard_map.95
  24.2 1.1 %shard_map.96.chip = f32[520,512]{1,0:T(8,128)S(1)} custom-call(f32[520,512]{1,0:T(8,128)S(1)} %collective-permute-done.1.early, f32[520,512]{1,0:T(8,128)S(1)} %shard_map.92.refs_0_.late.last), custom_call_target="tpu_custom_call" | custom-call | tf_op jit(solution)/shard_map/pallas_call | solution.py:336
  25.3 0.2 shard_map.98
  25.4 1.3 %collective-permute-start.4 = (f32[1,512]{1,0:T(1,128)S(1)}, f32[1,512]{1,0:T(1,128)S(1)}, u32[]{:S(2)}, u32[]{:S(2)}) collective-permute-start(f32[1,512]{1,0:T(1,128)S(1)} %get-tuple-element.34), channel_id=1, source_target_pairs={{0,2},{1,3},{2,0},{3,1},{4,6},{5,7},{6,4},{7,5},{8,10},{9,11},{10,... | collective-permute-start | bytes 6152 | tf_op jit(solution)/shard_map/ppermute | solution.py:361
  26.7 1.2 %collective-permute-done.4.moved = f32[1,512]{1,0:T(1,128)S(1)} collective-permute-done((f32[1,512]{1,0:T(1,128)S(1)}, f32[1,512]{1,0:T(1,128)S(1)}, u32[]{:S(2)}, u32[]{:S(2)}) %collective-permute-start.4) | collective-permute-done | bytes 2080 | tf_op jit(solution)/shard_map/ppermute | solution.py:361
  27.9 0.2 shard_map.99
  28.1 0.7 %collective-permute-start.5 = (f32[1,512]{1,0:T(1,128)S(1)}, f32[1,512]{1,0:T(1,128)S(1)}, u32[]{:S(2)}, u32[]{:S(2)}) collective-permute-start(f32[1,512]{1,0:T(1,128)S(1)} %get-tuple-element.36), channel_id=1, source_target_pairs={{7,9},{23,25}} | collective-permute-start | bytes 6152 | tf_op jit(solution)/shard_map/ppermute | solution.py:363
  28.8 0.2 shard_map.100
  28.9 1.3 %collective-permute-start.6 = (f32[1,512]{1,0:T(1,128)S(1)}, f32[1,512]{1,0:T(1,128)S(1)}, u32[]{:S(2)}, u32[]{:S(2)}) collective-permute-start(f32[1,512]{1,0:T(1,128)S(1)} %get-tuple-element.38), channel_id=1, source_target_pairs={{0,2},{1,3},{2,0},{3,1},{4,6},{5,7},{6,4},{7,5},{8,10},{9,11},{10,... | collective-permute-start | bytes 6152 | tf_op jit(solution)/shard_map/ppermute | solution.py:361
  30.2 1.2 %collective-permute-done.6.moved = f32[1,512]{1,0:T(1,128)S(1)} collective-permute-done((f32[1,512]{1,0:T(1,128)S(1)}, f32[1,512]{1,0:T(1,128)S(1)}, u32[]{:S(2)}, u32[]{:S(2)}) %collective-permute-start.6) | collective-permute-done | bytes 2080 | tf_op jit(solution)/shard_map/ppermute | solution.py:361
  31.4 0.2 shard_map.101
  31.6 1.3 %collective-permute-start.7 = (f32[1,512]{1,0:T(1,128)S(1)}, f32[1,512]{1,0:T(1,128)S(1)}, u32[]{:S(2)}, u32[]{:S(2)}) collective-permute-start(f32[1,512]{1,0:T(1,128)S(1)} %get-tuple-element.40), channel_id=1, source_target_pairs={{11,13},{27,29}} | collective-permute-start | bytes 6152 | tf_op jit(solution)/shard_map/ppermute | solution.py:363
  32.9 5.6 %collective-permute-done.7.moved = f32[1,512]{1,0:T(1,128)S(1)} collective-permute-done((f32[1,512]{1,0:T(1,128)S(1)}, f32[1,512]{1,0:T(1,128)S(1)}, u32[]{:S(2)}, u32[]{:S(2)}) %collective-permute-start.7) | collective-permute-done | bytes 2080 | tf_op jit(solution)/shard_map/ppermute | solution.py:363
  38.5 0.2 shard_map.102
  38.7 0.1 collective-permute-start.8
  38.7 0.1 collective-permute-start.10
  38.8 2.3 %collective-permute-done.8.moved = f32[1,512]{1,0:T(1,128)S(1)} collective-permute-done((f32[1,512]{1,0:T(1,128)S(1)}, f32[1,512]{1,0:T(1,128)S(1)}, u32[]{:S(2)}, u32[]{:S(2)}) %collective-permute-start.8) | collective-permute-done | bytes 2080 | tf_op jit(solution)/shard_map/ppermute | solution.py:361
  41.2 1.3 %shard_map.104.refs_0_ = f32[4,512]{1,0:T(4,128)} custom-call(f32[520,512]{1,0:T(8,128)S(1)} %collective-permute-done.1.early, f32[3,512,512]{2,1,0:T(8,128)S(1)} %get-tuple-element.28.steps, f32[520,512]{1,0:T(8,128)S(1)} %shard_map.92.refs_0_.late.last, f32[4,512]{1,0:T(4,128)S(1)} %get-tuple-element.29.refs_0_.free, f32[4,512]{1,0:T(4,128)S(1)} %get-tuple-element.30.mean, ...), custom_call_target="tpu_custom_call" | custom-call | tf_op jit(solution)/shard_map/pallas_call | solution.py:348
  (15 shorter events, 0.1 us)
Async XLA Ops:
  17.9 2.1 %collective-permute-start = (f32[1,512]{1,0:T(1,128)}, f32[1,512]{1,0:T(1,128)S(1)}, u32[]{:S(2)}, u32[]{:S(2)}) collective-permute-start(f32[1,512]{1,0:T(1,128)} %get-tuple-element.25), channel_id=1, source_target_pairs={{0,1},{1,0},{2,3},{3,2},{4,5},{5,4},{6,7},{7,6},{8,9},{9,8},{10,11... | collective-permute-start | bytes 6152 | tf_op jit(solution)/shard_map/ppermute | solution.py:325
  18.7 1.2 %copy-start.1 = (f32[520,512]{1,0:T(8,128)S(1)}, f32[520,512]{1,0:T(8,128)}, u32[]{:S(2)}) copy-start(f32[520,512]{1,0:T(8,128)} %get-tuple-element.24.refs_0_) | copy-start | bytes 3194884
  20.1 2.8 %copy-start.3 = (f32[512]{0:T(512)S(1)}, f32[512]{0:T(512)}, u32[]{:S(2)}) copy-start(f32[512]{0:T(512)} %param.13) | copy-start | bytes 6148
  20.1 2.8 %collective-permute-start.1 = (f32[520,512]{1,0:T(8,128)S(1)}, f32[520,512]{1,0:T(8,128)S(1)}, u32[]{:S(2)}, u32[]{:S(2)}) collective-permute-start(f32[520,512]{1,0:T(8,128)S(1)} %shard_map.93), channel_id=1, source_target_pairs={{0,1},{1,0},{2,3},{3,2},{4,5},{5,4},{6,7},{7,6},{8,9},{9,8},{10,11... | collective-permute-start | bytes 3194888 | tf_op jit(solution)/shard_map/ppermute | solution.py:328
  20.2 3.7 %copy-start = (f32[3,512,512]{2,1,0:T(8,128)S(1)}, f32[3,512,512]{2,1,0:T(8,128)}, u32[]{:S(2)}) copy-start(f32[3,512,512]{2,1,0:T(8,128)} %get-tuple-element.26.refs_0_) | copy-start | bytes 9437188
  20.4 3.5 %copy-start.2 = (f32[4,512]{1,0:T(4,128)S(1)}, f32[4,512]{1,0:T(4,128)}, u32[]{:S(2)}) copy-start(f32[4,512]{1,0:T(4,128)} %refs_2_.1) | copy-start | bytes 24580
  20.4 3.5 %copy-start.4 = (f32[4,512]{1,0:T(4,128)S(1)}, f32[4,512]{1,0:T(4,128)}, u32[]{:S(2)}) copy-start(f32[4,512]{1,0:T(4,128)} %get-tuple-element.27.refs_1_) | copy-start | bytes 24580
  20.4 2.5 %collective-permute-start.2 = (f32[1,512]{1,0:T(1,128)S(1)}, f32[1,512]{1,0:T(1,128)S(1)}, u32[]{:S(2)}, u32[]{:S(2)}) collective-permute-start(f32[1,512]{1,0:T(1,128)S(1)} %shard_map.94), channel_id=1, source_target_pairs={{0,2},{1,3},{2,0},{3,1},{4,6},{5,7},{6,4},{7,5},{8,10},{9,11},{10,... | collective-permute-start | bytes 6152 | tf_op jit(solution)/shard_map/ppermute | solution.py:361
  23.2 2.0 %collective-permute-start.3 = (f32[1,512]{1,0:T(1,128)S(1)}, f32[1,512]{1,0:T(1,128)S(1)}, u32[]{:S(2)}, u32[]{:S(2)}) collective-permute-start(f32[1,512]{1,0:T(1,128)S(1)} %get-tuple-element.32), channel_id=1, source_target_pairs={{3,5},{19,21}} | collective-permute-start | bytes 6152 | tf_op jit(solution)/shard_map/ppermute | solution.py:363
  25.4 2.5 %collective-permute-start.4 = (f32[1,512]{1,0:T(1,128)S(1)}, f32[1,512]{1,0:T(1,128)S(1)}, u32[]{:S(2)}, u32[]{:S(2)}) collective-permute-start(f32[1,512]{1,0:T(1,128)S(1)} %get-tuple-element.34), channel_id=1, source_target_pairs={{0,2},{1,3},{2,0},{3,1},{4,6},{5,7},{6,4},{7,5},{8,10},{9,11},{10,... | collective-permute-start | bytes 6152 | tf_op jit(solution)/shard_map/ppermute | solution.py:361
  28.1 0.7 %collective-permute-start.5 = (f32[1,512]{1,0:T(1,128)S(1)}, f32[1,512]{1,0:T(1,128)S(1)}, u32[]{:S(2)}, u32[]{:S(2)}) collective-permute-start(f32[1,512]{1,0:T(1,128)S(1)} %get-tuple-element.36), channel_id=1, source_target_pairs={{7,9},{23,25}} | collective-permute-start | bytes 6152 | tf_op jit(solution)/shard_map/ppermute | solution.py:363
  28.9 2.5 %collective-permute-start.6 = (f32[1,512]{1,0:T(1,128)S(1)}, f32[1,512]{1,0:T(1,128)S(1)}, u32[]{:S(2)}, u32[]{:S(2)}) collective-permute-start(f32[1,512]{1,0:T(1,128)S(1)} %get-tuple-element.38), channel_id=1, source_target_pairs={{0,2},{1,3},{2,0},{3,1},{4,6},{5,7},{6,4},{7,5},{8,10},{9,11},{10,... | collective-permute-start | bytes 6152 | tf_op jit(solution)/shard_map/ppermute | solution.py:361
  31.6 6.9 %collective-permute-start.7 = (f32[1,512]{1,0:T(1,128)S(1)}, f32[1,512]{1,0:T(1,128)S(1)}, u32[]{:S(2)}, u32[]{:S(2)}) collective-permute-start(f32[1,512]{1,0:T(1,128)S(1)} %get-tuple-element.40), channel_id=1, source_target_pairs={{11,13},{27,29}} | collective-permute-start | bytes 6152 | tf_op jit(solution)/shard_map/ppermute | solution.py:363
  38.7 2.5 %collective-permute-start.8 = (f32[1,512]{1,0:T(1,128)S(1)}, f32[1,512]{1,0:T(1,128)S(1)}, u32[]{:S(2)}, u32[]{:S(2)}) collective-permute-start(f32[1,512]{1,0:T(1,128)S(1)} %get-tuple-element.42), channel_id=1, source_target_pairs={{0,2},{1,3},{2,0},{3,1},{4,6},{5,7},{6,4},{7,5},{8,10},{9,11},{10,... | collective-permute-start | bytes 6152 | tf_op jit(solution)/shard_map/ppermute | solution.py:361
  38.7 2.4 %collective-permute-start.10 = (f32[1,512]{1,0:T(1,128)S(1)}, f32[1,512]{1,0:T(1,128)S(1)}, u32[]{:S(2)}, u32[]{:S(2)}) collective-permute-start(f32[1,512]{1,0:T(1,128)S(1)} %get-tuple-element.41.held.entry), channel_id=1, source_target_pairs={{0,1},{1,0},{2,3},{3,2},{4,5},{5,4},{6,7},{7,6},{8,9},{9,8},{10,11... | collective-permute-start | bytes 6152 | tf_op jit(solution)/shard_map/ppermute | solution.py:384
  41.2 1.3 %collective-permute-start.9 = (f32[1,512]{1,0:T(1,128)S(1)}, f32[1,512]{1,0:T(1,128)S(1)}, u32[]{:S(2)}, u32[]{:S(2)}) collective-permute-start(f32[1,512]{1,0:T(1,128)S(1)} %shard_map.103.entry), channel_id=1, source_target_pairs={{0,1},{1,0},{2,3},{3,2},{4,5},{5,4},{6,7},{7,6},{8,9},{9,8},{10,11... | collective-permute-start | bytes 6152 | tf_op jit(solution)/shard_map/ppermute | solution.py:393

commit v5 on v4

--- a/solution.py
+++ b/solution.py
@@ -30,38 +30,35 @@
     return both[:rows] + both[rows:] + jnp.dot(lhi, rlo, preferred_element_type=F32)
 
 
-def columns_of(row):
+def rows_times(row, *matrices):
     width = row.shape[1]
+    totals = [[None] * (width // LANES) for _ in matrices]
+    for b in range(0, width, LANES):
+        column = jnp.transpose(jnp.broadcast_to(row[:, b : b + LANES], (LANES, LANES)))
+        for total, matrix in zip(totals, matrices):
+            for i, c in enumerate(range(0, width, LANES)):
+                block = column * matrix(pl.ds(b, LANES), pl.ds(c, LANES))
+                term = jnp.sum(block.reshape(LANES // 8, 8, LANES), axis=0)
+                total[i] = term if total[i] is None else total[i] + term
     return [
-        jnp.transpose(jnp.broadcast_to(row[:, b : b + LANES], (LANES, LANES)))
-        for b in range(0, width, LANES)
+        jnp.concatenate([jnp.sum(part, axis=0, keepdims=True) for part in total], axis=1) for total in totals
     ]
 
 
-def row_times(cols, matrix):
-    width = len(cols) * LANES
-    parts = []
-    for c in range(0, width, LANES):
-        total = None
-        for b in range(len(cols)):
-            term = jnp.sum(
-                (cols[b] * matrix(pl.ds(b * LANES, LANES), pl.ds(c, LANES))).reshape(LANES // 8, 8, LANES),
-                axis=0,
-            )
-            total = term if total is None else total + term
-        parts.append(jnp.sum(total, axis=0, keepdims=True))
-    return jnp.concatenate(parts, axis=1)
+def row_times(row, matrix):
+    return rows_times(row, matrix)[0]
 
 
 def net_kernel(
     mean_h, spread_h, keep_h, obs_h, b_in_h, b_out_h, start_h, w_in_h, w_out_h,
-    steps, last, free, first,
+    prefix, last, offsets, first,
     mean_ref, spread_ref, keep_ref, obs_ref, b_in, b_out, start, w_in, w_out,
     turned, w_wide, base, wide, h0, h1, jac, pm, known_ref, held_ref, sems, out_sems,
 ):
     n_steps, width = mean_ref.shape
     units = w_in.shape[1]
-    half = width // 2
+    half = width // 4
+    per = width // half
     factor = math.sqrt(width + 1.0)
     sources = (mean_h, spread_h, keep_h, obs_h, b_in_h, b_out_h, start_h)
     targets = (mean_ref, spread_ref, keep_ref, obs_ref, b_in, b_out, start)
@@ -102,7 +99,7 @@
                 block = jnp.broadcast_to(turned[pl.ds(b, LANES), at : at + 1], (LANES, LANES))
                 if a == 3:
                     block = jnp.where(eye, block, 0.0)
-                wide[a, k, pl.ds(b, LANES), :] = block
+                wide[k][a // 2][a % 2, pl.ds(b, LANES), :] = block
 
     widen(0, (0, 1))
 
@@ -125,7 +122,7 @@
                 else:
                     w = w_wide[place]
                 for s in range(2):
-                    d = wide[s, k, pl.ds(j0 + r, 16), :]
+                    d = wide[k][0][s, pl.ds(j0 + r, 16), :]
                     y = b + jnp.concatenate([d, d], axis=1) * w
                     z = y * (y * y * (8.0 * C1) + 2.0 * C0)
                     dst[pl.ds(s * half + r, 16), pl.ds(c, 256)] = (y * jnp.tanh(z) + y).astype(BF16)
@@ -137,38 +134,42 @@
         for c in range(0, width, LANES):
             upper, lower = out[:half, c : c + LANES], out[half:, c : c + LANES]
             for r in range(0, half, LANES):
-                v = (upper[r : r + LANES] - lower[r : r + LANES]) * wide[2, k, pl.ds(j0 + r, LANES), :]
+                v = (upper[r : r + LANES] - lower[r : r + LANES]) * wide[k][1][0, pl.ds(j0 + r, LANES), :]
                 if c == j0 + r:
-                    v = v + wide[3, k, pl.ds(c, LANES), :]
-                jac[k, pl.ds(j0 + r, LANES), pl.ds(c, LANES)] = v * keep[:, c : c + LANES]
+                    v = v + wide[k][1][1, pl.ds(c, LANES), :]
+                jac[k][pl.ds(j0 + r, LANES), pl.ds(c, LANES)] = v * keep[:, c : c + LANES]
             sums.append(jnp.sum(upper + lower, axis=0, keepdims=True))
         return jnp.concatenate(sums, axis=1)
 
     sends = []
 
     def compose(k):
-        held = product(held_ref[k - 1] if k > 1 else jac[0], jac[k])
+        held = product((held_ref[k - 1] if k > 1 else jac[0])[...], jac[k][...])
         if k < n_steps - 1:
-            held_ref[k] = held
+            held_ref[k][...] = held
         else:
             last[pl.ds(0, width), :] = held
 
+    def send(k):
+        source = held_ref[k] if k > 0 else jac[0]
+        sends.append(pltpu.make_async_copy(source, prefix.at[k], out_sems.at[k]))
+        sends[-1].start()
+
     points = 2.0 * width
     slots = (h0, h1)
-    tiles = 2 * n_steps
+    tiles = per * n_steps
     for tile in range(tiles + 1):
         if tile == tiles - 1:
-            for k in range(n_steps - 1):
-                sends.append(pltpu.make_async_copy(jac.at[k], steps.at[k], out_sems.at[k]))
-                sends[-1].start()
+            for k in range(n_steps - 2):
+                send(k)
         if tile > 0:
-            k, side = (tile - 1) // 2, (tile - 1) % 2
-            total = outer(k, side * half, slots[side])
+            k, side = (tile - 1) // per, (tile - 1) % per
+            total = outer(k, side * half, slots[(tile - 1) % 2])
             pm[pl.ds(k, 1), :] = total if side == 0 else pm[pl.ds(k, 1), :] + total
-        if tile >= 5 and tile % 2 == 1:
-            compose((tile - 3) // 2)
+        if tile > 2 * per and tile % per == 1:
+            compose(tile // per - 1)
         if tile < tiles:
-            gelu(tile // 2, (tile % 2) * half, slots[tile % 2])
+            gelu(tile // per, (tile % per) * half, slots[tile % 2])
         if tile == 0:
             widen(0, (2, 3))
         if tile == 2:
@@ -182,18 +183,18 @@
                 + (points * b_out[...] + ((points - 2.0) * centre_f + (up + lo))) / (2.0 * (width + 1.0))
             ) + (1.0 - keep) * obs_ref[...]
             known_ref[pl.ds(0, n_steps), :] = known
-        if tile % 2 == 0 and tile + 2 < tiles:
-            widen(tile // 2 + 1, (0, 1, 2, 3))
-    for k in range((tiles - 3) // 2 + 1, n_steps):
-        compose(k)
+        if tile % per == 1 and tile + per < tiles:
+            widen(tile // per + 1, (0, 1, 2, 3))
+    send(n_steps - 2)
+    compose(n_steps - 1)
     const = jnp.zeros((1, width), F32)
     for k in range(n_steps):
         row = pl.ds(k, 1)
         own = known_ref[row, :] + keep_ref[row, :] * (pm[row, :] / (2.0 * (width + 1.0)))
-        free[row, :] = own
-        const = row_times(columns_of(const - mean_ref[row, :]), lambda r, c: jac[k, r, c]) + own
+        const = row_times(const - mean_ref[row, :], lambda r, c: jac[k][r, c]) + own
+        offsets[row, :] = const
     last[pl.ds(width, 8), :] = jnp.concatenate([const, jnp.zeros((7, width), F32)], axis=0)
-    first[...] = row_times(columns_of(start[...]), lambda r, c: last[r, c]) + const
+    first[...] = row_times(start[...], lambda r, c: last[r, c]) + const
     for send in sends:
         send.wait()
 
@@ -223,15 +224,15 @@
 
 def first_kernel(late, entry, leaving):
     width = late.shape[1]
-    leaving[...] = row_times(columns_of(entry[...]), lambda r, c: late[r, c]) + late[pl.ds(width, 1), :]
+    leaving[...] = row_times(entry[...], lambda r, c: late[r, c]) + late[pl.ds(width, 1), :]
 
 
 def second_kernel(early, late, held, moved, entry, leaving):
     width = late.shape[1]
     row = jnp.where(lax.axis_index("tm") == 3, moved[...], held[...])
     entry[...] = row
-    mid = row_times(columns_of(row), lambda r, c: early[r, c]) + early[pl.ds(width, 1), :]
-    leaving[...] = row_times(columns_of(mid), lambda r, c: late[r, c]) + late[pl.ds(width, 1), :]
+    mid = row_times(row, lambda r, c: early[r, c]) + early[pl.ds(width, 1), :]
+    leaving[...] = row_times(mid, lambda r, c: late[r, c]) + late[pl.ds(width, 1), :]
 
 
 def pair_kernel(early, late, chip):
@@ -248,29 +249,25 @@
     arrived = lax.axis_index("tm") == 2 * chip_at + 1
     row = jnp.where(arrived, moved[...], held[...])
     entry[...] = row
-    leaving[...] = row_times(columns_of(row), lambda r, c: chip[r, c]) + chip[pl.ds(width, 1), :]
+    leaving[...] = row_times(row, lambda r, c: chip[r, c]) + chip[pl.ds(width, 1), :]
 
 
 def arrive_kernel(chip_at, held, moved, entry):
     entry[...] = jnp.where(lax.axis_index("tm") == 2 * chip_at + 1, moved[...], held[...])
 
 
-def final_kernel(chosen, early, steps, last, free, mean, entry, other, *refs):
+def final_kernel(chosen, early, prefix, last, offsets, entry, other, *refs):
     out, rows, sem = refs[-3:]
-    n_steps, width = free.shape
+    n_steps, width = offsets.shape
     place = lax.axis_index("tm")
 
     @pl.when(chosen(place // 2))
     def _():
-        mid = row_times(columns_of(entry[...]), lambda r, c: early[r, c]) + early[pl.ds(width, 1), :]
+        mid = row_times(entry[...], lambda r, c: early[r, c]) + early[pl.ds(width, 1), :]
         state = jnp.where(place % 2 == 1, mid, other[...])
-        rows[pl.ds(n_steps - 1, 1), :] = (
-            row_times(columns_of(state), lambda r, c: last[r, c]) + last[pl.ds(width, 1), :]
-        )
-        for k in range(n_steps - 1):
-            row = pl.ds(k, 1)
-            state = row_times(columns_of(state - mean[row, :]), lambda r, c: steps[k, r, c]) + free[row, :]
-            rows[row, :] = state
+        loads = [lambda r, c, k=k: prefix[k, r, c] for k in range(n_steps - 1)]
+        moved = rows_times(state, *loads, lambda r, c: last[r, c])
+        rows[...] = jnp.concatenate(moved, axis=0) + offsets[...]
         copy = pltpu.make_async_copy(rows, out, sem)
         copy.start()
         copy.wait()
@@ -288,7 +285,7 @@
 
     small = pltpu.VMEM((n_steps, width), F32)
     row = start.reshape(1, width)
-    steps, last, free, first = pl.pallas_call(
+    prefix, last, offsets, first = pl.pallas_call(
         net_kernel,
         out_shape=(
             shape((n_steps - 1, width, width), F32),
@@ -308,13 +305,13 @@
             pltpu.VMEM((width, LANES), F32),
             pltpu.VMEM((width, units), F32),
             pltpu.VMEM((n_steps, units), F32),
-            pltpu.VMEM((4, n_steps, width, LANES), F32),
-            pltpu.VMEM((width, units), BF16),
-            pltpu.VMEM((width, units), BF16),
-            pltpu.VMEM((n_steps, width, width), F32),
+            [[pltpu.VMEM((2, width, LANES), F32)] * 2] * n_steps,
+            pltpu.VMEM((width // 2, units), BF16),
+            pltpu.VMEM((width // 2, units), BF16),
+            [pltpu.VMEM((width, width), F32)] * n_steps,
             pltpu.VMEM((8, width), F32),
             pltpu.VMEM((8, width), F32),
-            pltpu.VMEM((n_steps - 1, width, width), F32),
+            [pltpu.VMEM((width, width), F32)] * (n_steps - 1),
             pltpu.SemaphoreType.DMA((12,)),
             pltpu.SemaphoreType.DMA((n_steps,)),
         ],
@@ -348,12 +345,12 @@
         return pl.pallas_call(
             functools.partial(final_kernel, chosen),
             out_shape=shape((n_steps, width), F32),
-            in_specs=[VMEM] * 7 + [HBM] * len(kept),
+            in_specs=[VMEM] * 6 + [HBM] * len(kept),
             out_specs=HBM,
-            input_output_aliases={7: 0} if kept else {},
+            input_output_aliases={6: 0} if kept else {},
             scratch_shapes=[pltpu.VMEM((n_steps, width), F32), pltpu.SemaphoreType.DMA],
             compiler_params=params(16),
-        )(early, steps, late, free, lin_mean, entry, other, *kept)
+        )(early, prefix, late, offsets, entry, other, *kept)
 
     entry = row
     for chip_at in range(1, chips):
@@ -361,9 +358,9 @@
             moved = lax.ppermute(leaving, "tm", [(i, i ^ 2) for i in range(size)])
         else:
             moved = lax.ppermute(leaving, "tm", [(2 * chip_at - 1, 2 * chip_at + 1)])
-        ready = (free,) if chip_at == 2 else ()
+        ready = (offsets,) if chip_at == 2 else ()
         if chip_at == 1:
-            steps, free, lin_mean = fetch((steps, free, lin_mean), (moved,))
+            prefix, offsets = fetch((prefix, offsets), (moved,))
         if chip_at == 1 and chips > 2:
             entry, leaving = pl.pallas_call(
                 second_kernel,

time: 42.9 us -> 42.8 us (level)
    unnamed x10 -> x8, local copies, waits for them, and re-layouts: 1.25 us -> 1.25 us
  transfers between devices with their start and end apart: 11 -> 11, of which waited for: 5 -> 5; matrix products, arithmetic and copies ran while one was open for 0% -> 0% of each run, Pallas kernels for 7% -> 6%
where the time goes in v5:
time: 42.8 us; the launch traced here: 42.6 us
  Pallas kernels  21.9 us (51%)
  waiting for transfers between devices  11.6 us (27%)
  starting transfers between devices  7.5 us (18%)
  local copies, waits for them, and re-layouts  1.25 us (3%)
    pallas_call x1, Pallas kernels, body(): pl.pallas_call(net_kernel, out_shape=(shape((n_steps - 1, width, width),...  18 us
    ppermute x4, waiting for transfers between devices, body(): moved = lax.ppermute(leaving, 'tm', [(i, i ^ 2) for i in range(size)])  5.93 us
    ppermute x3, waiting for transfers between devices, body(): moved = lax.ppermute(leaving, 'tm', [(2 * chip_at - 1, 2 * chip_at + 1)])  5.61 us
    ppermute x4, starting transfers between devices, body(): moved = lax.ppermute(leaving, 'tm', [(i, i ^ 2) for i in range(size)])  3.98 us
    ppermute x3, starting transfers between devices, body(): moved = lax.ppermute(leaving, 'tm', [(2 * chip_at - 1, 2 * chip_at + 1)])  2.62 us
    unnamed x8, local copies, waits for them, and re-layouts  1.25 us
    pallas_call x2, Pallas kernels, finish(): pl.pallas_call(functools.partial(final_kernel, chosen), out_shape=shape((...  1.24 us
    pallas_call x1, Pallas kernels, body(): pl.pallas_call(pair_kernel, out_shape=shape((width + 8, width), F32), in_...  1.05 us
  transfers between devices with their start and end apart: 11, of which 5 were waited for; matrix products, arithmetic and copies ran while one was open for 0% of the time, Pallas kernels for 6%

profile of v5, /device:TPU:27, one launch (start us, length us, event | category | flops | bytes accessed | tf_op | source)
XLA Modules:
  0.0 42.6 jit_solution(11456818036661184812)
XLA Ops:
  0.0 18.0 %shard_map.91 = (f32[3,512,512]{2,1,0:T(8,128)}, f32[520,512]{1,0:T(8,128)}, f32[4,512]{1,0:T(4,128)}, f32[1,512]{1,0:T(1,128)}) custom-call(f32[4,512]{1,0:T(4,128)} %mean_h.1, f32[4,512]{1,0:T(4,128)} %spread_h.1, f32[4,512]{1,0:T(4,128)} %keep_h.1, f32[4,512]{1,0:T(4,128)} %obs_h.1, f32[1,2048]{1,0:T(1,128)} %bitcast.5, f32[1,512]{1,0:T(1,128)} %bitcast.6, ...), custom_call_target="tpu_custom_call" | custom-call | tf_op jit(solution)/shard_map/pallas_call | solution.py:288
  18.0 0.7 %collective-permute-start = (f32[1,512]{1,0:T(1,128)}, f32[1,512]{1,0:T(1,128)S(1)}, u32[]{:S(2)}, u32[]{:S(2)}) collective-permute-start(f32[1,512]{1,0:T(1,128)} %get-tuple-element.24), channel_id=1, source_target_pairs={{0,1},{1,0},{2,3},{3,2},{4,5},{5,4},{6,7},{7,6},{8,9},{9,8},{10,11... | collective-permute-start | bytes 6152 | tf_op jit(solution)/shard_map/ppermute | solution.py:322
  18.7 1.2 %copy-done.1 = f32[520,512]{1,0:T(8,128)S(1)} copy-done((f32[520,512]{1,0:T(8,128)S(1)}, f32[520,512]{1,0:T(8,128)}, u32[]{:S(2)}) %copy-start.1) | copy-done | bytes 1064984
  20.0 0.1 shard_map.92.refs_0_.late.last
  20.1 0.0 collective-permute-done.refs_1_.entry
  20.1 0.1 shard_map.93
  20.2 0.0 copy-start.2
  20.2 0.1 collective-permute-start.1
  20.3 0.1 shard_map.94
  20.4 0.0 copy-start.3
  20.5 1.3 %collective-permute-start.2 = (f32[1,512]{1,0:T(1,128)S(1)}, f32[1,512]{1,0:T(1,128)S(1)}, u32[]{:S(2)}, u32[]{:S(2)}) collective-permute-start(f32[1,512]{1,0:T(1,128)S(1)} %shard_map.94), channel_id=1, source_target_pairs={{0,2},{1,3},{2,0},{3,1},{4,6},{5,7},{6,4},{7,5},{8,10},{9,11},{10,... | collective-permute-start | bytes 6152 | tf_op jit(solution)/shard_map/ppermute | solution.py:358
  21.8 1.2 %collective-permute-done.2.refs_2_.moved = f32[1,512]{1,0:T(1,128)S(1)} collective-permute-done((f32[1,512]{1,0:T(1,128)S(1)}, f32[1,512]{1,0:T(1,128)S(1)}, u32[]{:S(2)}, u32[]{:S(2)}) %collective-permute-start.2) | collective-permute-done | bytes 2080 | tf_op jit(solution)/shard_map/ppermute | solution.py:358
  23.0 0.3 shard_map.97
  23.3 0.7 %collective-permute-start.3 = (f32[1,512]{1,0:T(1,128)S(1)}, f32[1,512]{1,0:T(1,128)S(1)}, u32[]{:S(2)}, u32[]{:S(2)}) collective-permute-start(f32[1,512]{1,0:T(1,128)S(1)} %get-tuple-element.30), channel_id=1, source_target_pairs={{3,5},{19,21}} | collective-permute-start | bytes 6152 | tf_op jit(solution)/shard_map/ppermute | solution.py:360
  24.0 0.2 shard_map.95
  24.2 1.0 %shard_map.96.chip = f32[520,512]{1,0:T(8,128)S(1)} custom-call(f32[520,512]{1,0:T(8,128)S(1)} %collective-permute-done.1.early, f32[520,512]{1,0:T(8,128)S(1)} %shard_map.92.refs_0_.late.last), custom_call_target="tpu_custom_call" | custom-call | tf_op jit(solution)/shard_map/pallas_call | solution.py:333
  25.3 0.2 shard_map.98
  25.4 1.3 %collective-permute-start.4 = (f32[1,512]{1,0:T(1,128)S(1)}, f32[1,512]{1,0:T(1,128)S(1)}, u32[]{:S(2)}, u32[]{:S(2)}) collective-permute-start(f32[1,512]{1,0:T(1,128)S(1)} %get-tuple-element.32), channel_id=1, source_target_pairs={{0,2},{1,3},{2,0},{3,1},{4,6},{5,7},{6,4},{7,5},{8,10},{9,11},{10,... | collective-permute-start | bytes 6152 | tf_op jit(solution)/shard_map/ppermute | solution.py:358
  26.7 1.2 %collective-permute-done.4.moved = f32[1,512]{1,0:T(1,128)S(1)} collective-permute-done((f32[1,512]{1,0:T(1,128)S(1)}, f32[1,512]{1,0:T(1,128)S(1)}, u32[]{:S(2)}, u32[]{:S(2)}) %collective-permute-start.4) | collective-permute-done | bytes 2080 | tf_op jit(solution)/shard_map/ppermute | solution.py:358
  27.9 0.2 shard_map.99
  28.1 0.7 %collective-permute-start.5 = (f32[1,512]{1,0:T(1,128)S(1)}, f32[1,512]{1,0:T(1,128)S(1)}, u32[]{:S(2)}, u32[]{:S(2)}) collective-permute-start(f32[1,512]{1,0:T(1,128)S(1)} %get-tuple-element.34), channel_id=1, source_target_pairs={{7,9},{23,25}} | collective-permute-start | bytes 6152 | tf_op jit(solution)/shard_map/ppermute | solution.py:360
  28.8 0.2 shard_map.100
  28.9 1.3 %collective-permute-start.6 = (f32[1,512]{1,0:T(1,128)S(1)}, f32[1,512]{1,0:T(1,128)S(1)}, u32[]{:S(2)}, u32[]{:S(2)}) collective-permute-start(f32[1,512]{1,0:T(1,128)S(1)} %get-tuple-element.36), channel_id=1, source_target_pairs={{0,2},{1,3},{2,0},{3,1},{4,6},{5,7},{6,4},{7,5},{8,10},{9,11},{10,... | collective-permute-start | bytes 6152 | tf_op jit(solution)/shard_map/ppermute | solution.py:358
  30.2 1.2 %collective-permute-done.6.moved = f32[1,512]{1,0:T(1,128)S(1)} collective-permute-done((f32[1,512]{1,0:T(1,128)S(1)}, f32[1,512]{1,0:T(1,128)S(1)}, u32[]{:S(2)}, u32[]{:S(2)}) %collective-permute-start.6) | collective-permute-done | bytes 2080 | tf_op jit(solution)/shard_map/ppermute | solution.py:358
  31.4 0.2 shard_map.101
  31.6 1.3 %collective-permute-start.7 = (f32[1,512]{1,0:T(1,128)S(1)}, f32[1,512]{1,0:T(1,128)S(1)}, u32[]{:S(2)}, u32[]{:S(2)}) collective-permute-start(f32[1,512]{1,0:T(1,128)S(1)} %get-tuple-element.38), channel_id=1, source_target_pairs={{11,13},{27,29}} | collective-permute-start | bytes 6152 | tf_op jit(solution)/shard_map/ppermute | solution.py:360
  32.9 5.6 %collective-permute-done.7.moved = f32[1,512]{1,0:T(1,128)S(1)} collective-permute-done((f32[1,512]{1,0:T(1,128)S(1)}, f32[1,512]{1,0:T(1,128)S(1)}, u32[]{:S(2)}, u32[]{:S(2)}) %collective-permute-start.7) | collective-permute-done | bytes 2080 | tf_op jit(solution)/shard_map/ppermute | solution.py:360
  38.5 0.2 shard_map.102
  38.7 0.1 collective-permute-start.8
  38.7 0.1 collective-permute-start.10
  38.8 2.3 %collective-permute-done.8.moved = f32[1,512]{1,0:T(1,128)S(1)} collective-permute-done((f32[1,512]{1,0:T(1,128)S(1)}, f32[1,512]{1,0:T(1,128)S(1)}, u32[]{:S(2)}, u32[]{:S(2)}) %collective-permute-start.8) | collective-permute-done | bytes 2080 | tf_op jit(solution)/shard_map/ppermute | solution.py:358
  41.2 1.2 %shard_map.104.refs_0_ = f32[4,512]{1,0:T(4,128)} custom-call(f32[520,512]{1,0:T(8,128)S(1)} %collective-permute-done.1.early, f32[3,512,512]{2,1,0:T(8,128)S(1)} %get-tuple-element.27.prefix, f32[520,512]{1,0:T(8,128)S(1)} %shard_map.92.refs_0_.late.last, f32[4,512]{1,0:T(4,128)S(1)} %get-tuple-element.28.refs_0_.offsets, ...), custom_call_target="tpu_custom_call" | custom-call | tf_op jit(solution)/shard_map/pallas_call | solution.py:345
  (13 shorter events, 0.1 us)
Async XLA Ops:
  18.0 2.1 %collective-permute-start = (f32[1,512]{1,0:T(1,128)}, f32[1,512]{1,0:T(1,128)S(1)}, u32[]{:S(2)}, u32[]{:S(2)}) collective-permute-start(f32[1,512]{1,0:T(1,128)} %get-tuple-element.24), channel_id=1, source_target_pairs={{0,1},{1,0},{2,3},{3,2},{4,5},{5,4},{6,7},{7,6},{8,9},{9,8},{10,11... | collective-permute-start | bytes 6152 | tf_op jit(solution)/shard_map/ppermute | solution.py:322
  18.7 1.2 %copy-start.1 = (f32[520,512]{1,0:T(8,128)S(1)}, f32[520,512]{1,0:T(8,128)}, u32[]{:S(2)}) copy-start(f32[520,512]{1,0:T(8,128)} %get-tuple-element.23.refs_0_) | copy-start | bytes 3194884
  20.2 2.8 %copy-start.2 = (f32[512]{0:T(512)S(1)}, f32[512]{0:T(512)}, u32[]{:S(2)}) copy-start(f32[512]{0:T(512)} %param.13) | copy-start | bytes 6148
  20.2 2.8 %collective-permute-start.1 = (f32[520,512]{1,0:T(8,128)S(1)}, f32[520,512]{1,0:T(8,128)S(1)}, u32[]{:S(2)}, u32[]{:S(2)}) collective-permute-start(f32[520,512]{1,0:T(8,128)S(1)} %shard_map.93), channel_id=1, source_target_pairs={{0,1},{1,0},{2,3},{3,2},{4,5},{5,4},{6,7},{7,6},{8,9},{9,8},{10,11... | collective-permute-start | bytes 3194888 | tf_op jit(solution)/shard_map/ppermute | solution.py:325
  20.3 3.7 %copy-start = (f32[3,512,512]{2,1,0:T(8,128)S(1)}, f32[3,512,512]{2,1,0:T(8,128)}, u32[]{:S(2)}) copy-start(f32[3,512,512]{2,1,0:T(8,128)} %get-tuple-element.25.refs_0_) | copy-start | bytes 9437188
  20.4 3.5 %copy-start.3 = (f32[4,512]{1,0:T(4,128)S(1)}, f32[4,512]{1,0:T(4,128)}, u32[]{:S(2)}) copy-start(f32[4,512]{1,0:T(4,128)} %get-tuple-element.26.refs_1_) | copy-start | bytes 24580
  20.5 2.5 %collective-permute-start.2 = (f32[1,512]{1,0:T(1,128)S(1)}, f32[1,512]{1,0:T(1,128)S(1)}, u32[]{:S(2)}, u32[]{:S(2)}) collective-permute-start(f32[1,512]{1,0:T(1,128)S(1)} %shard_map.94), channel_id=1, source_target_pairs={{0,2},{1,3},{2,0},{3,1},{4,6},{5,7},{6,4},{7,5},{8,10},{9,11},{10,... | collective-permute-start | bytes 6152 | tf_op jit(solution)/shard_map/ppermute | solution.py:358
  23.3 2.0 %collective-permute-start.3 = (f32[1,512]{1,0:T(1,128)S(1)}, f32[1,512]{1,0:T(1,128)S(1)}, u32[]{:S(2)}, u32[]{:S(2)}) collective-permute-start(f32[1,512]{1,0:T(1,128)S(1)} %get-tuple-element.30), channel_id=1, source_target_pairs={{3,5},{19,21}} | collective-permute-start | bytes 6152 | tf_op jit(solution)/shard_map/ppermute | solution.py:360
  25.4 2.5 %collective-permute-start.4 = (f32[1,512]{1,0:T(1,128)S(1)}, f32[1,512]{1,0:T(1,128)S(1)}, u32[]{:S(2)}, u32[]{:S(2)}) collective-permute-start(f32[1,512]{1,0:T(1,128)S(1)} %get-tuple-element.32), channel_id=1, source_target_pairs={{0,2},{1,3},{2,0},{3,1},{4,6},{5,7},{6,4},{7,5},{8,10},{9,11},{10,... | collective-permute-start | bytes 6152 | tf_op jit(solution)/shard_map/ppermute | solution.py:358
  28.1 0.7 %collective-permute-start.5 = (f32[1,512]{1,0:T(1,128)S(1)}, f32[1,512]{1,0:T(1,128)S(1)}, u32[]{:S(2)}, u32[]{:S(2)}) collective-permute-start(f32[1,512]{1,0:T(1,128)S(1)} %get-tuple-element.34), channel_id=1, source_target_pairs={{7,9},{23,25}} | collective-permute-start | bytes 6152 | tf_op jit(solution)/shard_map/ppermute | solution.py:360
  28.9 2.5 %collective-permute-start.6 = (f32[1,512]{1,0:T(1,128)S(1)}, f32[1,512]{1,0:T(1,128)S(1)}, u32[]{:S(2)}, u32[]{:S(2)}) collective-permute-start(f32[1,512]{1,0:T(1,128)S(1)} %get-tuple-element.36), channel_id=1, source_target_pairs={{0,2},{1,3},{2,0},{3,1},{4,6},{5,7},{6,4},{7,5},{8,10},{9,11},{10,... | collective-permute-start | bytes 6152 | tf_op jit(solution)/shard_map/ppermute | solution.py:358
  31.6 6.9 %collective-permute-start.7 = (f32[1,512]{1,0:T(1,128)S(1)}, f32[1,512]{1,0:T(1,128)S(1)}, u32[]{:S(2)}, u32[]{:S(2)}) collective-permute-start(f32[1,512]{1,0:T(1,128)S(1)} %get-tuple-element.38), channel_id=1, source_target_pairs={{11,13},{27,29}} | collective-permute-start | bytes 6152 | tf_op jit(solution)/shard_map/ppermute | solution.py:360
  38.7 2.5 %collective-permute-start.8 = (f32[1,512]{1,0:T(1,128)S(1)}, f32[1,512]{1,0:T(1,128)S(1)}, u32[]{:S(2)}, u32[]{:S(2)}) collective-permute-start(f32[1,512]{1,0:T(1,128)S(1)} %get-tuple-element.40), channel_id=1, source_target_pairs={{0,2},{1,3},{2,0},{3,1},{4,6},{5,7},{6,4},{7,5},{8,10},{9,11},{10,... | collective-permute-start | bytes 6152 | tf_op jit(solution)/shard_map/ppermute | solution.py:358
  38.7 2.4 %collective-permute-start.10 = (f32[1,512]{1,0:T(1,128)S(1)}, f32[1,512]{1,0:T(1,128)S(1)}, u32[]{:S(2)}, u32[]{:S(2)}) collective-permute-start(f32[1,512]{1,0:T(1,128)S(1)} %get-tuple-element.39.held.entry), channel_id=1, source_target_pairs={{0,1},{1,0},{2,3},{3,2},{4,5},{5,4},{6,7},{7,6},{8,9},{9,8},{10,11... | collective-permute-start | bytes 6152 | tf_op jit(solution)/shard_map/ppermute | solution.py:381
  41.2 1.2 %collective-permute-start.9 = (f32[1,512]{1,0:T(1,128)S(1)}, f32[1,512]{1,0:T(1,128)S(1)}, u32[]{:S(2)}, u32[]{:S(2)}) collective-permute-start(f32[1,512]{1,0:T(1,128)S(1)} %shard_map.103.entry), channel_id=1, source_target_pairs={{0,1},{1,0},{2,3},{3,2},{4,5},{5,4},{6,7},{7,6},{8,9},{9,8},{10,11... | collective-permute-start | bytes 6152 | tf_op jit(solution)/shard_map/ppermute | solution.py:390
